TPU v7x, 256 devices: a whole 4x4x8 slice. The times are simulated.
256 devices in a mesh: dp: 8 (over z), ctx: 32 (over x, y, core).
Axes of the slice: x: 4, y: 4, z: 8, core: 2. Of those that a mesh axis runs over, the one named last changes fastest.
Arguments:
- queries: bfloat16 [16, 4096, 512], P('dp', 'ctx'), may hold values from -40 to 40
- keys: bfloat16 [16, 4096, 128], P('dp', 'ctx'), may hold values from -18 to 18
- values: bfloat16 [16, 4096, 128], P('dp', 'ctx'), may hold values from -6 to 6
- upstream: bfloat16 [16, 4096, 512], P('dp', 'ctx'), may hold values from -6 to 6
- doc_ids: int32 [16, 4096], P('dp'), may hold values from 0 to 31, as said below
Outputs:
- attn_out: bfloat16 [16, 4096, 512], P('dp', 'ctx')
- grad_query: bfloat16 [16, 4096, 512], P('dp', 'ctx')
- grad_key: bfloat16 [16, 4096, 128], P('dp', 'ctx')
- grad_value: bfloat16 [16, 4096, 128], P('dp', 'ctx')
Inputs may be any that keep to these rules, and one draw needn't show every extreme that they name: `doc_ids`: ids never fall along a pack; document 0 holds exactly 256 tokens and every other document 1 to 256 tokens.
All inputs are finite; a program needn't handle non-finite values.
Results may differ from a plain program's by a relative error of at most 0.013.
Values may be sent and summed in bfloat16 or wider, within the bound.
A program may use at most 64 MiB of HBM per device.

v0:
```python
import jax
import jax.numpy as jnp
from jax import lax
from jax.sharding import PartitionSpec as P

MOST = 256


NEG_LARGE = -1e30


def from_behind(value, axis, steps):
    count = lax.axis_size(axis)
    initial, last = (max(0, -steps), min(count, count - steps))
    return lax.ppermute(value, axis, [(source, source + steps) for source in range(initial, last)])


def swapped_2(block, axis, bit):
    count = lax.axis_size(axis)
    route = []
    for low in range(count):
        high = low | 1 << bit
        if high != low and high < count:
            route += [(low, high), (high, low)]
    return lax.ppermute(block, axis, route)


def passed_along(value, axis, by):
    count = lax.axis_size(axis)
    return lax.ppermute(value, axis, [(i, (i + by) % count) for i in range(count)])


def pack_costs(doc_ids, tok_rows):
    firsts = doc_ids[:, ::tok_rows]
    finals = doc_ids[:, tok_rows - 1 :: tok_rows]
    blocks = firsts.shape[1]
    block_order = jnp.arange(blocks, dtype=jnp.int32)
    earlier = block_order[None, :] < block_order[:, None]
    linked = (finals[:, None, :] == firsts[:, :, None]) & earlier[None, :, :]
    return jnp.sum(linked.astype(jnp.int32), axis=(1, 2)) + blocks


def tile_mask(doc_ids, query_ids, query_pos, source, tok_rows):
    first_row = source * tok_rows
    key_ids = lax.dynamic_slice_in_dim(doc_ids, first_row, tok_rows, 1)
    key_pos = first_row + jnp.arange(tok_rows, dtype=jnp.int32)
    same_doc = query_ids[:, :, None] == key_ids[:, None, :]
    causal = key_pos[None, :] <= query_pos[:, None]
    return same_doc & causal[None, :, :]


def forward_tile(running, query_heads, upward, key_blk, value_blk, pairs, score_scale):
    row_peak, row_total, weighted = running
    allowed = pairs[:, None, :, :]
    scores = (
        jnp.einsum("pthd,psd->phts", query_heads, key_blk, preferred_element_type=jnp.float32)
        * score_scale
    )
    masked = jnp.where(allowed, scores, NEG_LARGE)
    new_peak = jnp.maximum(row_peak, jnp.max(masked, axis=-1))
    factor = jnp.exp(row_peak - new_peak)
    weights = jnp.exp(masked - new_peak[..., None])
    slopes = jnp.einsum("pthd,psd->phts", upward, value_blk, preferred_element_type=jnp.float32)
    row_total = row_total * factor + jnp.sum(weights, axis=-1)
    weighted = weighted * factor + jnp.sum(weights * slopes, axis=-1)
    return (new_peak, row_total, weighted)


def backward_tile(
    accums, query_heads, upward, key_blk, value_blk, pairs, log_total, row_delta, score_scale
):
    out_acc, query_acc, key_acc, value_acc = accums
    allowed = pairs[:, None, :, :]
    scores = (
        jnp.einsum("pthd,psd->phts", query_heads, key_blk, preferred_element_type=jnp.float32)
        * score_scale
    )
    masked = jnp.where(allowed, scores, NEG_LARGE)
    prob = jnp.where(allowed, jnp.exp(masked - log_total[..., None]), 0.0)
    prob_low = prob.astype(jnp.bfloat16)
    slopes = jnp.einsum("pthd,psd->phts", upward, value_blk, preferred_element_type=jnp.float32)
    dscore_low = (prob * (slopes - row_delta[..., None])).astype(jnp.bfloat16)
    out_acc = out_acc + jnp.einsum(
        "phts,psd->pthd", prob_low, value_blk, preferred_element_type=jnp.float32
    )
    query_acc = query_acc + jnp.einsum(
        "phts,psd->pthd", dscore_low, key_blk, preferred_element_type=jnp.float32
    )
    key_acc = key_acc + jnp.einsum(
        "phts,pthd->psd", dscore_low, query_heads, preferred_element_type=jnp.float32
    )
    value_acc = value_acc + jnp.einsum(
        "phts,pthd->psd", prob_low, upward, preferred_element_type=jnp.float32
    )
    return (out_acc, query_acc, key_acc, value_acc)


def relay_keys(keys_now, values_now):
    return from_behind((keys_now, values_now), "ctx", 1)


def per_device(queries, keys, values, upstream, doc_ids):
    pack_count, tok_rows, feature_all = queries.shape
    head_dim = keys.shape[2]
    head_count = feature_all // head_dim
    score_scale = head_dim ** (-0.5)
    ctx_size = lax.axis_size("ctx")
    reach_turns = MOST // tok_rows
    trades = []
    pack_load = pack_costs(doc_ids, tok_rows)
    for bit_index in range(lax.axis_size("dp").bit_length() - 1):
        swapped = swapped_2(
            (queries[1], keys[1], values[1], upstream[1], doc_ids[1], pack_load), "dp", bit_index
        )
        other_load = swapped[5]
        before = jnp.maximum(pack_load[0] + pack_load[1], other_load[0] + other_load[1])
        balanced = jnp.maximum(pack_load[0] + other_load[1], other_load[0] + pack_load[1])
        traded = balanced < before
        queries = queries.at[1].set(jnp.where(traded, swapped[0], queries[1]))
        keys = keys.at[1].set(jnp.where(traded, swapped[1], keys[1]))
        values = values.at[1].set(jnp.where(traded, swapped[2], values[1]))
        upstream = upstream.at[1].set(jnp.where(traded, swapped[3], upstream[1]))
        doc_ids = doc_ids.at[1].set(jnp.where(traded, swapped[4], doc_ids[1]))
        pack_load = jnp.stack([pack_load[0], jnp.where(traded, other_load[1], pack_load[1])])
        trades.append(traded)
    own_block = lax.axis_index("ctx")
    query_ids = lax.dynamic_slice_in_dim(doc_ids, own_block * tok_rows, tok_rows, 1)
    query_pos = own_block * tok_rows + jnp.arange(tok_rows, dtype=jnp.int32)
    query_heads = queries.reshape(pack_count, tok_rows, head_count, head_dim)
    upward = upstream.reshape(pack_count, tok_rows, head_count, head_dim)
    stat_shape = (pack_count, head_count, tok_rows)
    local_pairs = tile_mask(doc_ids, query_ids, query_pos, own_block, tok_rows)
    running = (
        jnp.full(stat_shape, NEG_LARGE, jnp.float32),
        jnp.zeros(stat_shape, jnp.float32),
        jnp.zeros(stat_shape, jnp.float32),
    )
    running = forward_tile(running, query_heads, upward, keys, values, local_pairs, score_scale)
    store_depth = 1
    key_store = jnp.zeros((store_depth,) + keys.shape, keys.dtype)
    value_store = jnp.zeros((store_depth,) + values.shape, values.dtype)

    def forward_turn(position, carried):
        keys_now, values_now, running, key_store, value_store = carried
        keys_now, values_now = relay_keys(keys_now, values_now)
        source = (own_block - position) % ctx_size
        pairs = tile_mask(doc_ids, query_ids, query_pos, source, tok_rows)
        running = lax.cond(
            jnp.any(pairs),
            lambda current: forward_tile(
                current, query_heads, upward, keys_now, values_now, pairs, score_scale
            ),
            lambda current: current,
            running,
        )
        return (keys_now, values_now, running, key_store, value_store)

    carried = lax.fori_loop(
        1, reach_turns + 1, forward_turn, (keys, values, running, key_store, value_store)
    )
    row_peak, row_total, weighted = carried[2]
    key_store = carried[3]
    value_store = carried[4]
    log_total = row_peak + jnp.log(row_total)
    row_delta = weighted / row_total
    zeros_query = jnp.zeros((pack_count, tok_rows, head_count, head_dim), jnp.float32)
    zeros_key = jnp.zeros(keys.shape, jnp.float32)
    accums = backward_tile(
        (zeros_query, zeros_query, zeros_key, zeros_key),
        query_heads,
        upward,
        keys,
        values,
        local_pairs,
        log_total,
        row_delta,
        score_scale,
    )

    def backward_turn(position, carried):
        keys_now, values_now, accums = carried
        out_acc, query_acc, key_acc, value_acc = accums
        key_acc, value_acc = (
            passed_along(key_acc.astype(jnp.bfloat16), "ctx", 1).astype(key_acc.dtype),
            passed_along(value_acc.astype(jnp.bfloat16), "ctx", 1).astype(value_acc.dtype),
        )
        keys_now, values_now = relay_keys(keys_now, values_now)
        source = (own_block - position) % ctx_size
        pairs = tile_mask(doc_ids, query_ids, query_pos, source, tok_rows)
        accums = lax.cond(
            jnp.any(pairs),
            lambda current: backward_tile(
                current,
                query_heads,
                upward,
                keys_now,
                values_now,
                pairs,
                log_total,
                row_delta,
                score_scale,
            ),
            lambda current: current,
            (out_acc, query_acc, key_acc, value_acc),
        )
        return (keys_now, values_now, accums)

    carried = lax.fori_loop(1, reach_turns + 1, backward_turn, (keys, values, accums))
    out_acc, query_acc, key_acc, value_acc = carried[2]
    key_acc, value_acc = (
        passed_along(key_acc.astype(jnp.bfloat16), "ctx", -reach_turns).astype(key_acc.dtype),
        passed_along(value_acc.astype(jnp.bfloat16), "ctx", -reach_turns).astype(value_acc.dtype),
    )
    attn_out = out_acc.reshape(pack_count, tok_rows, feature_all).astype(jnp.bfloat16)
    grad_query = (
        (query_acc * score_scale).reshape(pack_count, tok_rows, feature_all).astype(jnp.bfloat16)
    )
    grad_key = (key_acc * score_scale).astype(jnp.bfloat16)
    grad_value = value_acc.astype(jnp.bfloat16)
    for bit_index in reversed(range(len(trades))):
        returned = swapped_2(
            (attn_out[1], grad_query[1], grad_key[1], grad_value[1]), "dp", bit_index
        )
        traded = trades[bit_index]
        attn_out = attn_out.at[1].set(jnp.where(traded, returned[0], attn_out[1]))
        grad_query = grad_query.at[1].set(jnp.where(traded, returned[1], grad_query[1]))
        grad_key = grad_key.at[1].set(jnp.where(traded, returned[2], grad_key[1]))
        grad_value = grad_value.at[1].set(jnp.where(traded, returned[3], grad_value[1]))
    return (attn_out, grad_query, grad_key, grad_value)


def solution(mesh):
    return jax.shard_map(
        per_device,
        mesh=mesh,
        in_specs=(
            P("dp", "ctx", None),
            P("dp", "ctx", None),
            P("dp", "ctx", None),
            P("dp", "ctx", None),
            P("dp", None),
        ),
        out_specs=(
            P("dp", "ctx", None),
            P("dp", "ctx", None),
            P("dp", "ctx", None),
            P("dp", "ctx", None),
        ),
        check_vma=False,
    )
```

profile of v0, /device:TPU:2, one launch (start us, length us, event | category | flops | bytes accessed | tf_op | source)
XLA Modules:
  0.0 189.9 jit_solution(10316757306113703944)
XLA Ops:
  18.4 3.3 %collective-permute-start.8 = (s32[2]{0:T(128)S(1)}, s32[2]{0:T(128)S(1)}, u32[]{:S(2)}, u32[]{:S(2)}) collective-permute-start(s32[2]{0:T(128)S(1)} %pad_add_fusion), channel_id=1, source_target_pairs={{0,64},{64,0},{32,96},{96,32},{128,192},{192,128},{160,224},{224,1... | collective-permute-start | bytes 32 | tf_op jit(solution)/shard_map/ppermute | solution.py:25
  28.8 6.0 %collective-permute-start.10 = (s32[2]{0:T(128)S(1)}, s32[2]{0:T(128)S(1)}, u32[]{:S(2)}, u32[]{:S(2)}) collective-permute-start(s32[2]{0:T(128)S(1)} %pad_add_fusion.1), channel_id=1, source_target_pairs={{0,128},{128,0},{32,160},{160,32},{64,192},{192,64},{96,224},{224,... | collective-permute-start | bytes 32 | tf_op jit(solution)/shard_map/ppermute | solution.py:25
  45.8 5.9 %collective-permute-start.17 = (s32[4096]{0:T(1024)S(1)}, s32[4096]{0:T(1024)S(1)}, u32[]{:S(2)}, u32[]{:S(2)}) collective-permute-start(s32[4096]{0:T(1024)S(1)} %broadcast_select_fusion.17), channel_id=1, source_target_pairs={{0,128},{128,0},{32,160},{160,32},{64,192},{192,64},{96,224},{224,... | collective-permute-start | bytes 49160 | tf_op jit(solution)/shard_map/ppermute | solution.py:25
  53.8 3.0 %collective-permute-done.13 = bf16[128,128]{1,0:T(8,128)(2,1)S(1)} collective-permute-done((bf16[128,128]{1,0:T(8,128)(2,1)S(1)}, bf16[128,128]{1,0:T(8,128)(2,1)S(1)}, u32[]{:S(2)}, u32[]{:S(2)}) %collective-permute-start.13) | collective-permute-done | bytes 32800 | tf_op jit(solution)/shard_map/ppermute | solution.py:25
  56.9 3.0 %collective-permute-start.14 = (bf16[128,128]{1,0:T(8,128)(2,1)S(1)}, bf16[128,128]{1,0:T(8,128)(2,1)S(1)}, u32[]{:S(2)}, u32[]{:S(2)}) collective-permute-start(bf16[128,128]{1,0:T(8,128)(2,1)S(1)} %get-tuple-element.1298), channel_id=1, source_target_pairs={{0,128},{128,0},{32,160},{160,32},{64,192},{192,64},{96,224},{224,... | collective-permute-start | bytes 98312 | tf_op jit(solution)/shard_map/ppermute | solution.py:25
  60.0 3.1 %collective-permute-start.11 = (bf16[128,128]{1,0:T(8,128)(2,1)S(1)}, bf16[128,128]{1,0:T(8,128)(2,1)S(1)}, u32[]{:S(2)}, u32[]{:S(2)}) collective-permute-start(bf16[128,128]{1,0:T(8,128)(2,1)S(1)} %get-tuple-element.1300), channel_id=1, source_target_pairs={{0,128},{128,0},{32,160},{160,32},{64,192},{192,64},{96,224},{224,... | collective-permute-start | bytes 98312 | tf_op jit(solution)/shard_map/ppermute | solution.py:25
  64.9 3.4 %collective-permute-done.11 = bf16[128,128]{1,0:T(8,128)(2,1)S(1)} collective-permute-done((bf16[128,128]{1,0:T(8,128)(2,1)S(1)}, bf16[128,128]{1,0:T(8,128)(2,1)S(1)}, u32[]{:S(2)}, u32[]{:S(2)}) %collective-permute-start.11) | collective-permute-done | bytes 32800 | tf_op jit(solution)/shard_map/ppermute | solution.py:25
  71.5 12.6 %collective-permute-done.19 = bf16[128,512]{0,1:T(8,128)(2,1)S(1)} collective-permute-done((bf16[128,512]{0,1:T(8,128)(2,1)S(1)}, bf16[128,512]{0,1:T(8,128)(2,1)S(1)}, u32[]{:S(2)}, u32[]{:S(2)}) %collective-permute-start.19) | collective-permute-done | bytes 131104 | tf_op jit(solution)/shard_map/ppermute | solution.py:25
  84.2 3.1 %collective-permute-start.20 = (bf16[128,512]{0,1:T(8,128)(2,1)S(1)}, bf16[128,512]{0,1:T(8,128)(2,1)S(1)}, u32[]{:S(2)}, u32[]{:S(2)}) collective-permute-start(bf16[128,512]{0,1:T(8,128)(2,1)S(1)} %get-tuple-element.1296), channel_id=1, source_target_pairs={{0,128},{128,0},{32,160},{160,32},{64,192},{192,64},{96,224},{224,... | collective-permute-start | bytes 393224 | tf_op jit(solution)/shard_map/ppermute | solution.py:25
  87.3 3.2 %collective-permute-start.23 = (bf16[128,512]{0,1:T(8,128)(2,1)S(1)}, bf16[128,512]{0,1:T(8,128)(2,1)S(1)}, u32[]{:S(2)}, u32[]{:S(2)}) collective-permute-start(bf16[128,512]{0,1:T(8,128)(2,1)S(1)} %get-tuple-element.1294), channel_id=1, source_target_pairs={{0,128},{128,0},{32,160},{160,32},{64,192},{192,64},{96,224},{224,... | collective-permute-start | bytes 393224 | tf_op jit(solution)/shard_map/ppermute | solution.py:25
  90.5 3.7 %collective-permute-done.20 = bf16[128,512]{0,1:T(8,128)(2,1)S(1)} collective-permute-done((bf16[128,512]{0,1:T(8,128)(2,1)S(1)}, bf16[128,512]{0,1:T(8,128)(2,1)S(1)}, u32[]{:S(2)}, u32[]{:S(2)}) %collective-permute-start.20) | collective-permute-done | bytes 131104 | tf_op jit(solution)/shard_map/ppermute | solution.py:25
  97.2 20.0 %while.77 = (s32[]{:T(128)}, bf16[2,128,128]{2,1,0:T(8,128)(2,1)S(1)}, bf16[2,128,128]{2,1,0:T(8,128)(2,1)S(1)}, f32[2,4,128]{2,1,0:T(4,128)S(1)}, f32[2,4,128]{...) while((s32[]{:T(128)}, ...), condition=%wide.region_11.12_spmd.clone, body=%wide.region_4.11_spmd.clone.sunk | while | flops 68275472 | bytes 3193382 | solution.py:158
  99.2 3.6 %collective-permute-start.1 = (bf16[2,128,128]{2,1,0:T(8,128)(2,1)S(1)}, bf16[2,128,128]{2,1,0:T(8,128)(2,1)S(1)}, u32[]{:S(2)}, u32[]{:S(2)}) collective-permute-start(bf16[2,128,128]{2,1,0:T(8,128)(2,1)S(1)} %get-tuple-element.1544), channel_id=1, source_target_pairs={{0,1},{1,2},{2,3},{3,4},{4,5},{5,6},{6,7},{7,8},{8,9},{9,10},{10,1... | collective-permute-start | bytes 196616 | tf_op jit(solution)/shard_map/while/body/eval_jaxpr/ppermute | solution.py:15
  113.0 2.3 %collective-permute-done = bf16[2,128,128]{2,1,0:T(8,128)(2,1)S(1)} collective-permute-done((bf16[2,128,128]{2,1,0:T(8,128)(2,1)S(1)}, bf16[2,128,128]{2,1,0:T(8,128)(2,1)S(1)}, u32[]{:S(2)}, u32[]{:S(2)}) %collective-permute-start) | collective-permute-done | bytes 65568 | tf_op jit(solution)/shard_map/while/body/eval_jaxpr/ppermute | solution.py:15
  118.8 21.4 %while.78 = (s32[]{:T(128)}, bf16[2,128,128]{2,1,0:T(8,128)(2,1)S(1)}, bf16[2,128,128]{2,1,0:T(8,128)(2,1)S(1)}, f32[2,128,4,128]{3,1,2,0:T(8,128)S(1)}, f32[2,1...) while((s32[]{:T(128)}, ...), condition=%wide.region_16.17_spmd.clone, body=%wide.region_12.16_spmd.clone.sunk | while | flops 203079952 | bytes 9026230 | solution.py:208
  132.5 3.7 %collective-permute-start.3 = (bf16[2,128,128]{2,1,0:T(8,128)(2,1)S(1)}, bf16[2,128,128]{2,1,0:T(8,128)(2,1)S(1)}, u32[]{:S(2)}, u32[]{:S(2)}) collective-permute-start(bf16[2,128,128]{2,1,0:T(8,128)(2,1)S(1)} %get-tuple-element.1601), channel_id=1, source_target_pairs={{0,1},{1,2},{2,3},{3,4},{4,5},{5,6},{6,7},{7,8},{8,9},{9,10},{10,1... | collective-permute-start | bytes 196616 | tf_op jit(solution)/shard_map/while/body/eval_jaxpr/ppermute | solution.py:15
  143.0 4.7 %collective-permute-start.27 = (bf16[128,512]{0,1:T(8,128)(2,1)S(1)}, bf16[128,512]{0,1:T(8,128)(2,1)S(1)}, u32[]{:S(2)}, u32[]{:S(2)}) collective-permute-start(bf16[128,512]{0,1:T(8,128)(2,1)S(1)} %bitcast.251), channel_id=1, source_target_pairs={{0,128},{128,0},{32,160},{160,32},{64,192},{192,64},{96,224},{224,... | collective-permute-start | bytes 393224 | tf_op jit(solution)/shard_map/ppermute | solution.py:25
  149.3 4.7 %collective-permute-start.31 = (bf16[128,128]{1,0:T(8,128)(2,1)S(1)}, bf16[128,128]{1,0:T(8,128)(2,1)S(1)}, u32[]{:S(2)}, u32[]{:S(2)}) collective-permute-start(bf16[128,128]{1,0:T(8,128)(2,1)S(1)} %slice_bitcast_fusion.3), channel_id=1, source_target_pairs={{0,128},{128,0},{32,160},{160,32},{64,192},{192,64},{96,224},{224,... | collective-permute-start | bytes 98312 | tf_op jit(solution)/shard_map/ppermute | solution.py:25
  155.3 7.2 %collective-permute-done.31 = bf16[128,128]{1,0:T(8,128)(2,1)S(1)} collective-permute-done((bf16[128,128]{1,0:T(8,128)(2,1)S(1)}, bf16[128,128]{1,0:T(8,128)(2,1)S(1)}, u32[]{:S(2)}, u32[]{:S(2)}) %collective-permute-start.31) | collective-permute-done | bytes 32800 | tf_op jit(solution)/shard_map/ppermute | solution.py:25
  163.2 2.4 %collective-permute-start.36 = (bf16[128,128]{1,0:T(8,128)(2,1)S(1)}, bf16[128,128]{1,0:T(8,128)(2,1)S(1)}, u32[]{:S(2)}, u32[]{:S(2)}) collective-permute-start(bf16[128,128]{1,0:T(8,128)(2,1)S(1)} %broadcast_select_fusion.8), channel_id=1, source_target_pairs={{0,64},{64,0},{32,96},{96,32},{128,192},{192,128},{160,224},{224,1... | collective-permute-start | bytes 98312 | tf_op jit(solution)/shard_map/ppermute | solution.py:25
  165.7 2.4 %collective-permute-done.36 = bf16[128,128]{1,0:T(8,128)(2,1)S(1)} collective-permute-done((bf16[128,128]{1,0:T(8,128)(2,1)S(1)}, bf16[128,128]{1,0:T(8,128)(2,1)S(1)}, u32[]{:S(2)}, u32[]{:S(2)}) %collective-permute-start.36) | collective-permute-done | bytes 32800 | tf_op jit(solution)/shard_map/ppermute | solution.py:25
  170.4 2.7 %collective-permute-start.28 = (bf16[128,512]{0,1:T(8,128)(2,1)S(1)}, bf16[128,512]{0,1:T(8,128)(2,1)S(1)}, u32[]{:S(2)}, u32[]{:S(2)}) collective-permute-start(bf16[128,512]{0,1:T(8,128)(2,1)S(1)} %broadcast_select_fusion), channel_id=1, source_target_pairs={{0,64},{64,0},{32,96},{96,32},{128,192},{192,128},{160,224},{224,1... | collective-permute-start | bytes 393224 | tf_op jit(solution)/shard_map/ppermute | solution.py:25
  174.4 6.7 %collective-permute-done.28 = bf16[128,512]{0,1:T(8,128)(2,1)S(1)} collective-permute-done((bf16[128,512]{0,1:T(8,128)(2,1)S(1)}, bf16[128,512]{0,1:T(8,128)(2,1)S(1)}, u32[]{:S(2)}, u32[]{:S(2)}) %collective-permute-start.28) | collective-permute-done | bytes 131104 | tf_op jit(solution)/shard_map/ppermute | solution.py:25
  183.5 3.7 %collective-permute-done.29 = bf16[128,512]{0,1:T(8,128)(2,1)S(1)} collective-permute-done((bf16[128,512]{0,1:T(8,128)(2,1)S(1)}, bf16[128,512]{0,1:T(8,128)(2,1)S(1)}, u32[]{:S(2)}, u32[]{:S(2)}) %collective-permute-start.29) | collective-permute-done | bytes 131104 | tf_op jit(solution)/shard_map/ppermute | solution.py:25
  (233 shorter events, 79.3 us)
Async XLA Ops:
  2.8 8.8 %collective-permute-start.6 = (s32[2]{0:T(128)S(1)}, s32[2]{0:T(128)S(1)}, u32[]{:S(2)}, u32[]{:S(2)}) collective-permute-start(s32[2]{0:T(128)S(1)} %broadcast_add_fusion), channel_id=1, source_target_pairs={{0,32},{32,0},{64,96},{96,64},{128,160},{160,128},{192,224},{224,1... | collective-permute-start | bytes 32 | tf_op jit(solution)/shard_map/ppermute | solution.py:25
  5.0 63.3 %collective-permute-start.21 = (bf16[128,512]{0,1:T(8,128)(2,1)S(1)}, bf16[128,512]{0,1:T(8,128)(2,1)S(1)}, u32[]{:S(2)}, u32[]{:S(2)}) collective-permute-start(bf16[128,512]{0,1:T(8,128)(2,1)S(1)} %slice_bitcast_fusion), channel_id=1, source_target_pairs={{0,32},{32,0},{64,96},{96,64},{128,160},{160,128},{192,224},{224,1... | collective-permute-start | bytes 393224 | tf_op jit(solution)/shard_map/ppermute | solution.py:25
  5.2 35.7 %collective-permute-start.15 = (s32[4096]{0:T(1024)S(1)}, s32[4096]{0:T(1024)S(1)}, u32[]{:S(2)}, u32[]{:S(2)}) collective-permute-start(s32[4096]{0:T(1024)S(1)} %bitcast.268), channel_id=1, source_target_pairs={{0,32},{32,0},{64,96},{96,64},{128,160},{160,128},{192,224},{224,1... | collective-permute-start | bytes 49160 | tf_op jit(solution)/shard_map/ppermute | solution.py:25
  7.4 62.0 %collective-permute-start.18 = (bf16[128,512]{0,1:T(8,128)(2,1)S(1)}, bf16[128,512]{0,1:T(8,128)(2,1)S(1)}, u32[]{:S(2)}, u32[]{:S(2)}) collective-permute-start(bf16[128,512]{0,1:T(8,128)(2,1)S(1)} %slice_bitcast_fusion.1), channel_id=1, source_target_pairs={{0,32},{32,0},{64,96},{96,64},{128,160},{160,128},{192,224},{224,1... | collective-permute-start | bytes 393224 | tf_op jit(solution)/shard_map/ppermute | solution.py:25
  9.6 33.6 %collective-permute-start.7 = (bf16[128,128]{1,0:T(8,128)(2,1)S(1)}, bf16[128,128]{1,0:T(8,128)(2,1)S(1)}, u32[]{:S(2)}, u32[]{:S(2)}) collective-permute-start(bf16[128,128]{1,0:T(8,128)(2,1)S(1)} %slice_bitcast_fusion.5), channel_id=1, source_target_pairs={{0,32},{32,0},{64,96},{96,64},{128,160},{160,128},{192,224},{224,1... | collective-permute-start | bytes 98312 | tf_op jit(solution)/shard_map/ppermute | solution.py:25
  39.9 11.9 %collective-permute-start.12 = (bf16[128,128]{1,0:T(8,128)(2,1)S(1)}, bf16[128,128]{1,0:T(8,128)(2,1)S(1)}, u32[]{:S(2)}, u32[]{:S(2)}) collective-permute-start(bf16[128,128]{1,0:T(8,128)(2,1)S(1)} %slice_bitcast_fusion.4), channel_id=1, source_target_pairs={{0,32},{32,0},{64,96},{96,64},{128,160},{160,128},{192,224},{224,1... | collective-permute-start | bytes 98312 | tf_op jit(solution)/shard_map/ppermute | solution.py:25
  43.2 16.7 %collective-permute-start.9 = (bf16[128,128]{1,0:T(8,128)(2,1)S(1)}, bf16[128,128]{1,0:T(8,128)(2,1)S(1)}, u32[]{:S(2)}, u32[]{:S(2)}) collective-permute-start(bf16[128,128]{1,0:T(8,128)(2,1)S(1)} %broadcast_select_fusion.15), channel_id=1, source_target_pairs={{0,64},{64,0},{32,96},{96,32},{128,192},{192,128},{160,224},{224,1... | collective-permute-start | bytes 98312 | tf_op jit(solution)/shard_map/ppermute | solution.py:25
  45.8 7.7 %collective-permute-start.17 = (s32[4096]{0:T(1024)S(1)}, s32[4096]{0:T(1024)S(1)}, u32[]{:S(2)}, u32[]{:S(2)}) collective-permute-start(s32[4096]{0:T(1024)S(1)} %broadcast_select_fusion.17), channel_id=1, source_target_pairs={{0,128},{128,0},{32,160},{160,32},{64,192},{192,64},{96,224},{224,... | collective-permute-start | bytes 49160 | tf_op jit(solution)/shard_map/ppermute | solution.py:25
  56.9 7.9 %collective-permute-start.14 = (bf16[128,128]{1,0:T(8,128)(2,1)S(1)}, bf16[128,128]{1,0:T(8,128)(2,1)S(1)}, u32[]{:S(2)}, u32[]{:S(2)}) collective-permute-start(bf16[128,128]{1,0:T(8,128)(2,1)S(1)} %get-tuple-element.1298), channel_id=1, source_target_pairs={{0,128},{128,0},{32,160},{160,32},{64,192},{192,64},{96,224},{224,... | collective-permute-start | bytes 98312 | tf_op jit(solution)/shard_map/ppermute | solution.py:25
  60.0 8.3 %collective-permute-start.11 = (bf16[128,128]{1,0:T(8,128)(2,1)S(1)}, bf16[128,128]{1,0:T(8,128)(2,1)S(1)}, u32[]{:S(2)}, u32[]{:S(2)}) collective-permute-start(bf16[128,128]{1,0:T(8,128)(2,1)S(1)} %get-tuple-element.1300), channel_id=1, source_target_pairs={{0,128},{128,0},{32,160},{160,32},{64,192},{192,64},{96,224},{224,... | collective-permute-start | bytes 98312 | tf_op jit(solution)/shard_map/ppermute | solution.py:25
  68.4 18.9 %collective-permute-start.22 = (bf16[128,512]{0,1:T(8,128)(2,1)S(1)}, bf16[128,512]{0,1:T(8,128)(2,1)S(1)}, u32[]{:S(2)}, u32[]{:S(2)}) collective-permute-start(bf16[128,512]{0,1:T(8,128)(2,1)S(1)} %broadcast_select_fusion.6), channel_id=1, source_target_pairs={{0,64},{64,0},{32,96},{96,32},{128,192},{192,128},{160,224},{224,1... | collective-permute-start | bytes 393224 | tf_op jit(solution)/shard_map/ppermute | solution.py:25
  69.5 14.7 %collective-permute-start.19 = (bf16[128,512]{0,1:T(8,128)(2,1)S(1)}, bf16[128,512]{0,1:T(8,128)(2,1)S(1)}, u32[]{:S(2)}, u32[]{:S(2)}) collective-permute-start(bf16[128,512]{0,1:T(8,128)(2,1)S(1)} %broadcast_select_fusion.7), channel_id=1, source_target_pairs={{0,64},{64,0},{32,96},{96,32},{128,192},{192,128},{160,224},{224,1... | collective-permute-start | bytes 393224 | tf_op jit(solution)/shard_map/ppermute | solution.py:25
  84.2 10.1 %collective-permute-start.20 = (bf16[128,512]{0,1:T(8,128)(2,1)S(1)}, bf16[128,512]{0,1:T(8,128)(2,1)S(1)}, u32[]{:S(2)}, u32[]{:S(2)}) collective-permute-start(bf16[128,512]{0,1:T(8,128)(2,1)S(1)} %get-tuple-element.1296), channel_id=1, source_target_pairs={{0,128},{128,0},{32,160},{160,32},{64,192},{192,64},{96,224},{224,... | collective-permute-start | bytes 393224 | tf_op jit(solution)/shard_map/ppermute | solution.py:25
  87.3 9.4 %collective-permute-start.23 = (bf16[128,512]{0,1:T(8,128)(2,1)S(1)}, bf16[128,512]{0,1:T(8,128)(2,1)S(1)}, u32[]{:S(2)}, u32[]{:S(2)}) collective-permute-start(bf16[128,512]{0,1:T(8,128)(2,1)S(1)} %get-tuple-element.1294), channel_id=1, source_target_pairs={{0,128},{128,0},{32,160},{160,32},{64,192},{192,64},{96,224},{224,... | collective-permute-start | bytes 393224 | tf_op jit(solution)/shard_map/ppermute | solution.py:25
  119.1 7.7 %collective-permute-start.2 = (bf16[2,128,128]{2,1,0:T(8,128)(2,1)S(1)}, bf16[2,128,128]{2,1,0:T(8,128)(2,1)S(1)}, u32[]{:S(2)}, u32[]{:S(2)}) collective-permute-start(bf16[2,128,128]{2,1,0:T(8,128)(2,1)S(1)} %get-tuple-element.1600), channel_id=1, source_target_pairs={{0,1},{1,2},{2,3},{3,4},{4,5},{5,6},{6,7},{7,8},{8,9},{9,10},{10,1... | collective-permute-start | bytes 196616 | tf_op jit(solution)/shard_map/while/body/eval_jaxpr/ppermute | solution.py:15
  121.0 7.7 %collective-permute-start.3 = (bf16[2,128,128]{2,1,0:T(8,128)(2,1)S(1)}, bf16[2,128,128]{2,1,0:T(8,128)(2,1)S(1)}, u32[]{:S(2)}, u32[]{:S(2)}) collective-permute-start(bf16[2,128,128]{2,1,0:T(8,128)(2,1)S(1)} %get-tuple-element.1601), channel_id=1, source_target_pairs={{0,1},{1,2},{2,3},{3,4},{4,5},{5,6},{6,7},{7,8},{8,9},{9,10},{10,1... | collective-permute-start | bytes 196616 | tf_op jit(solution)/shard_map/while/body/eval_jaxpr/ppermute | solution.py:15
  140.4 8.9 %collective-permute-start.30 = (bf16[2,128,128]{2,1,0:T(8,128)(2,1)S(1)}, bf16[2,128,128]{2,1,0:T(8,128)(2,1)S(1)}, u32[]{:S(2)}, u32[]{:S(2)}) collective-permute-start(bf16[2,128,128]{2,1,0:T(8,128)(2,1)S(1)} %convert_element_type.108), channel_id=1, source_target_pairs={{0,30},{1,31},{2,0},{3,1},{4,2},{5,3},{6,4},{7,5},{8,6},{9,7},{10,... | collective-permute-start | bytes 196616 | tf_op jit(solution)/shard_map/ppermute | solution.py:30
  142.7 11.3 %collective-permute-start.34 = (bf16[2,128,128]{2,1,0:T(8,128)(2,1)S(1)}, bf16[2,128,128]{2,1,0:T(8,128)(2,1)S(1)}, u32[]{:S(2)}, u32[]{:S(2)}) collective-permute-start(bf16[2,128,128]{2,1,0:T(8,128)(2,1)S(1)} %convert_element_type.111), channel_id=1, source_target_pairs={{0,30},{1,31},{2,0},{3,1},{4,2},{5,3},{6,4},{7,5},{8,6},{9,7},{10,... | collective-permute-start | bytes 196616 | tf_op jit(solution)/shard_map/ppermute | solution.py:30
  143.0 27.3 %collective-permute-start.27 = (bf16[128,512]{0,1:T(8,128)(2,1)S(1)}, bf16[128,512]{0,1:T(8,128)(2,1)S(1)}, u32[]{:S(2)}, u32[]{:S(2)}) collective-permute-start(bf16[128,512]{0,1:T(8,128)(2,1)S(1)} %bitcast.251), channel_id=1, source_target_pairs={{0,128},{128,0},{32,160},{160,32},{64,192},{192,64},{96,224},{224,... | collective-permute-start | bytes 393224 | tf_op jit(solution)/shard_map/ppermute | solution.py:25
  147.8 25.4 %collective-permute-start.24 = (bf16[128,512]{0,1:T(8,128)(2,1)S(1)}, bf16[128,512]{0,1:T(8,128)(2,1)S(1)}, u32[]{:S(2)}, u32[]{:S(2)}) collective-permute-start(bf16[128,512]{0,1:T(8,128)(2,1)S(1)} %bitcast.250), channel_id=1, source_target_pairs={{0,128},{128,0},{32,160},{160,32},{64,192},{192,64},{96,224},{224,... | collective-permute-start | bytes 393224 | tf_op jit(solution)/shard_map/ppermute | solution.py:25
  149.3 13.2 %collective-permute-start.31 = (bf16[128,128]{1,0:T(8,128)(2,1)S(1)}, bf16[128,128]{1,0:T(8,128)(2,1)S(1)}, u32[]{:S(2)}, u32[]{:S(2)}) collective-permute-start(bf16[128,128]{1,0:T(8,128)(2,1)S(1)} %slice_bitcast_fusion.3), channel_id=1, source_target_pairs={{0,128},{128,0},{32,160},{160,32},{64,192},{192,64},{96,224},{224,... | collective-permute-start | bytes 98312 | tf_op jit(solution)/shard_map/ppermute | solution.py:25
  154.0 9.2 %collective-permute-start.35 = (bf16[128,128]{1,0:T(8,128)(2,1)S(1)}, bf16[128,128]{1,0:T(8,128)(2,1)S(1)}, u32[]{:S(2)}, u32[]{:S(2)}) collective-permute-start(bf16[128,128]{1,0:T(8,128)(2,1)S(1)} %slice_bitcast_fusion.2), channel_id=1, source_target_pairs={{0,128},{128,0},{32,160},{160,32},{64,192},{192,64},{96,224},{224,... | collective-permute-start | bytes 98312 | tf_op jit(solution)/shard_map/ppermute | solution.py:25
  170.4 10.6 %collective-permute-start.28 = (bf16[128,512]{0,1:T(8,128)(2,1)S(1)}, bf16[128,512]{0,1:T(8,128)(2,1)S(1)}, u32[]{:S(2)}, u32[]{:S(2)}) collective-permute-start(bf16[128,512]{0,1:T(8,128)(2,1)S(1)} %broadcast_select_fusion), channel_id=1, source_target_pairs={{0,64},{64,0},{32,96},{96,32},{128,192},{192,128},{160,224},{224,1... | collective-permute-start | bytes 393224 | tf_op jit(solution)/shard_map/ppermute | solution.py:25
  173.2 9.9 %collective-permute-start.25 = (bf16[128,512]{0,1:T(8,128)(2,1)S(1)}, bf16[128,512]{0,1:T(8,128)(2,1)S(1)}, u32[]{:S(2)}, u32[]{:S(2)}) collective-permute-start(bf16[128,512]{0,1:T(8,128)(2,1)S(1)} %broadcast_select_fusion.1), channel_id=1, source_target_pairs={{0,64},{64,0},{32,96},{96,32},{128,192},{192,128},{160,224},{224,1... | collective-permute-start | bytes 393224 | tf_op jit(solution)/shard_map/ppermute | solution.py:25
  (26 other events, 145.2 us)
where the time goes:
time: 190 us
  starting transfers between devices  84.9 us (45%)
  waiting for transfers between devices  68.7 us (36%)
  between operations  15.3 us (8%)
  local copies, waits for them, and re-layouts  7.8 us (4%)
  other arithmetic  6.38 us (3%)
  matrix products  3.57 us (2%)
  loops' own time  3.21 us (2%)
    ppermute x30, starting transfers between devices, swapped_2(): return lax.ppermute(block, axis, route)  63.3 us
    ppermute x30, waiting for transfers between devices, swapped_2(): return lax.ppermute(block, axis, route)  55.4 us
    ppermute x8, starting transfers between devices, from_behind(): lax.ppermute(value, axis, [(source, source + steps) for source in range(i...  18.8 us
    ppermute x8, waiting for transfers between devices, from_behind(): lax.ppermute(value, axis, [(source, source + steps) for source in range(i...  12.4 us
  transfers between devices with their start and end apart: 44, of which 27 were waited for; matrix products, arithmetic and copies ran while one was open for 5% of the time, Pallas kernels for 0%

commit v1 on v0

v1 whole, which is shorter than its diff:
```python
import math

import jax
import jax.numpy as jnp
from jax import lax
from jax.experimental import pallas as pl
from jax.experimental.pallas import tpu as pltpu
from jax.sharding import PartitionSpec as P

MESH = pl.DeviceIdType.MESH
NEG_LARGE = -1e30
HEAD = 128


def nt(a, b):
    return lax.dot_general(a, b, (((1,), (1,)), ((), ())), preferred_element_type=jnp.float32)


def nn(a, b):
    return lax.dot_general(a, b, (((1,), (0,)), ((), ())), preferred_element_type=jnp.float32)


def stacked(ref, block, heads):
    return jnp.concatenate(
        [ref[block, :, h * HEAD : (h + 1) * HEAD] for h in range(heads)], axis=0
    )


def kernel(
    q_hbm, k_hbm, v_hbm, u_hbm, ids_hbm,
    out_hbm, gq_hbm, gk_hbm, gv_hbm,
    q_all, u_all, k_all, v_all, ids_v, bias,
    e_loc, d_loc, p_low, s_low,
    gk_send, gv_send, gk_in, gv_in, gk_mate, gv_mate, gk_mine, gv_mine, gk_fin, gv_fin,
    out_buf, gq_buf,
    load_sem, ids_sem, kv_send, kv_recv, mate_send, mate_recv,
    g_send, g_recv, gm_send, gm_recv, o_send, o_recv, store_sem, fin_sem,
):
    tok = q_all.shape[1]
    heads = q_all.shape[2] // HEAD
    scale = HEAD**-0.5
    log2_scale = scale * math.log2(math.e)
    ctx = lax.axis_index("ctx")
    dp = lax.axis_index("dp")
    chips = lax.axis_size("ctx") // 2
    chip = ctx // 2
    core = ctx % 2
    peer = 1 - core
    mate = chip * 2 + peer
    later = lax.rem(chip + 1, chips)
    earlier = lax.rem(chip + chips - 1, chips)

    def remote(src, dst, send, recv, target):
        return pltpu.make_async_remote_copy(
            src_ref=src, dst_ref=dst, send_sem=send, recv_sem=recv,
            device_id=(dp, target), device_id_type=MESH,
        )

    barrier = pltpu.get_barrier_semaphore()
    for target in (earlier * 2, earlier * 2 + 1, mate):
        pl.semaphore_signal(barrier, inc=1, device_id=(dp, target), device_id_type=MESH)

    loads = [
        pltpu.make_async_copy(q_hbm.at[core], q_all.at[core], load_sem.at[0]),
        pltpu.make_async_copy(u_hbm.at[core], u_all.at[core], load_sem.at[1]),
        pltpu.make_async_copy(k_hbm.at[core], k_all.at[2 + core], load_sem.at[2]),
        pltpu.make_async_copy(v_hbm.at[core], v_all.at[2 + core], load_sem.at[3]),
        pltpu.make_async_copy(
            ids_hbm.at[:, pl.ds(pl.multiple_of(earlier * 2 * tok, 2 * tok), 2 * tok)],
            ids_v.at[:, pl.ds(0, 2 * tok)], ids_sem.at[0],
        ),
        pltpu.make_async_copy(
            ids_hbm.at[:, pl.ds(pl.multiple_of(chip * 2 * tok, 2 * tok), 2 * tok)],
            ids_v.at[:, pl.ds(2 * tok, 2 * tok)], ids_sem.at[1],
        ),
    ]
    for copy in loads:
        copy.start()

    pl.semaphore_wait(barrier, 3)

    kv_out = []
    for pack in range(2):
        target = later * 2 + pack
        kv_out += [
            remote(k_hbm.at[pack], k_all.at[core], kv_send.at[pack, 0], kv_recv.at[core, 0], target),
            remote(v_hbm.at[pack], v_all.at[core], kv_send.at[pack, 1], kv_recv.at[core, 1], target),
        ]
    mate_out = [
        remote(k_hbm.at[peer], k_all.at[2 + core], mate_send.at[0], mate_recv.at[0], mate),
        remote(v_hbm.at[peer], v_all.at[2 + core], mate_send.at[1], mate_recv.at[1], mate),
        remote(q_hbm.at[peer], q_all.at[core], mate_send.at[2], mate_recv.at[2], mate),
        remote(u_hbm.at[peer], u_all.at[core], mate_send.at[3], mate_recv.at[3], mate),
    ]
    for copy in kv_out + mate_out:
        copy.start()

    for copy in loads[4:]:
        copy.wait()
    ids_two = ids_v[...]
    ids_row = jnp.where(core == 0, ids_two[0:1], ids_two[1:2])
    lane = lax.broadcasted_iota(jnp.int32, ids_row.shape, 1)
    ids_row = jnp.where((lane < 2 * tok) & (chip == 0), -1, ids_row)
    ids_col = jnp.transpose(jnp.broadcast_to(ids_row, (tok, 4 * tok)))
    for block in range(2):
        first = block * tok
        q_first = (2 + block) * tok
        key_pos = first + lax.broadcasted_iota(jnp.int32, (3 * tok, tok), 0)
        query_pos = q_first + lax.broadcasted_iota(jnp.int32, (3 * tok, tok), 1)
        allowed = (ids_col[first : first + 3 * tok] == ids_row[:, q_first : q_first + tok]) & (
            key_pos <= query_pos
        )
        bias[block] = jnp.where(allowed, 0.0, NEG_LARGE)

    for copy in loads[:4]:
        copy.wait()
    mate_in = [
        remote(k_hbm.at[core], k_all.at[2 + peer], mate_send.at[0], mate_recv.at[0], mate),
        remote(v_hbm.at[core], v_all.at[2 + peer], mate_send.at[1], mate_recv.at[1], mate),
        remote(q_hbm.at[core], q_all.at[peer], mate_send.at[2], mate_recv.at[2], mate),
        remote(u_hbm.at[core], u_all.at[peer], mate_send.at[3], mate_recv.at[3], mate),
    ]
    for copy in mate_in:
        copy.wait_recv()

    def tile(block, key_first, key_blocks):
        span = key_blocks * tok
        keys = k_all[key_first : key_first + key_blocks].reshape(span, HEAD)
        vals = v_all[key_first : key_first + key_blocks].reshape(span, HEAD)
        row = (key_first - block) * tok
        add = bias[block, row : row + span]
        scores = nt(keys, stacked(q_all, block, heads))
        slopes = nt(vals, stacked(u_all, block, heads))
        scores = scores * log2_scale + jnp.concatenate([add] * heads, axis=1)
        return scores, slopes

    local = []
    for block in range(2):
        span = (block + 1) * tok
        scores, slopes = tile(block, 2, block + 1)
        peak = jnp.max(scores, axis=0, keepdims=True)
        weights = jnp.exp2(scores - peak)
        e_loc[block, :span] = weights
        d_loc[block, :span] = slopes
        total = jnp.sum(weights, axis=0, keepdims=True)
        weighted = jnp.sum(weights * slopes, axis=0, keepdims=True)
        local.append((peak, total, weighted))

    for block in range(2):
        for array in range(2):
            ref = (k_all, v_all)[array]
            remote(
                (k_hbm, v_hbm)[array].at[0], ref.at[block],
                kv_send.at[0, array], kv_recv.at[block, array], mate,
            ).wait_recv()

    stats = []
    back = []
    carry_k = carry_v = None
    for block in range(2):
        span = (2 - block) * tok
        scores, slopes = tile(block, block, 2 - block)
        peak, total, weighted = local[block]
        new_peak = jnp.maximum(peak, jnp.max(scores, axis=0, keepdims=True))
        factor = jnp.exp2(peak - new_peak)
        weights = jnp.exp2(scores - new_peak)
        total = total * factor + jnp.sum(weights, axis=0, keepdims=True)
        weighted = weighted * factor + jnp.sum(weights * slopes, axis=0, keepdims=True)
        inverse = 1.0 / total
        delta = weighted * inverse
        stats.append((factor * inverse, delta))
        prob = weights * inverse
        prob_b = prob.astype(jnp.bfloat16)
        slope_b = (prob * (slopes - delta)).astype(jnp.bfloat16)
        p_low[block, :span] = prob_b
        s_low[block, :span] = slope_b
        part_v = nn(prob_b, stacked(u_all, block, heads))
        part_k = nn(slope_b, stacked(q_all, block, heads))
        if block == 0:
            carry_k, carry_v = part_k[tok:], part_v[tok:]
            done_k, done_v = part_k[:tok], part_v[:tok]
        else:
            done_k, done_v = carry_k + part_k, carry_v + part_v
        gk_send[block] = done_k.astype(jnp.bfloat16)
        gv_send[block] = done_v.astype(jnp.bfloat16)
        target = earlier * 2 + block
        for copy in (
            remote(gk_send.at[block], gk_in.at[core], g_send.at[block, 0], g_recv.at[core, 0], target),
            remote(gv_send.at[block], gv_in.at[core], g_send.at[block, 1], g_recv.at[core, 1], target),
        ):
            copy.start()
            back.append(copy)

    for block in range(2):
        span = (block + 1) * tok
        row = (2 - block) * tok
        scaled, delta = stats[block]
        prob = e_loc[block, :span] * scaled
        prob_b = prob.astype(jnp.bfloat16)
        slope_b = (prob * (d_loc[block, :span] - delta)).astype(jnp.bfloat16)
        p_low[block, row:] = prob_b
        s_low[block, row:] = slope_b
        part_v = nn(prob_b, stacked(u_all, block, heads))
        part_k = nn(slope_b, stacked(q_all, block, heads))
        if block == 0:
            carry_k, carry_v = part_k, part_v
        else:
            gk_mine[0] = carry_k + part_k[:tok]
            gv_mine[0] = carry_v + part_v[:tok]
            gk_mine[1] = part_k[tok:]
            gv_mine[1] = part_v[tok:]
    mates = [
        remote(gk_mine.at[peer], gk_mate, gm_send.at[0], gm_recv.at[0], mate),
        remote(gv_mine.at[peer], gv_mate, gm_send.at[1], gm_recv.at[1], mate),
    ]
    for copy in mates:
        copy.start()

    for block in range(2):
        keys = k_all[block : block + 3].reshape(3 * tok, HEAD)
        vals = v_all[block : block + 3].reshape(3 * tok, HEAD)
        out_t = nn(jnp.transpose(vals), p_low[block]).astype(jnp.bfloat16)
        gq_t = (nn(jnp.transpose(keys), s_low[block]) * scale).astype(jnp.bfloat16)
        for h in range(heads):
            cols = slice(h * HEAD, (h + 1) * HEAD)
            rows = slice(h * tok, (h + 1) * tok)
            out_buf[block, :, cols] = jnp.transpose(out_t[:, rows])
            gq_buf[block, :, cols] = jnp.transpose(gq_t[:, rows])
    outs = [
        remote(out_buf.at[peer], out_hbm.at[core], o_send.at[0], o_recv.at[0], mate),
        remote(gq_buf.at[peer], gq_hbm.at[core], o_send.at[1], o_recv.at[1], mate),
    ]
    stores = [
        pltpu.make_async_copy(out_buf.at[core], out_hbm.at[core], store_sem.at[0]),
        pltpu.make_async_copy(gq_buf.at[core], gq_hbm.at[core], store_sem.at[1]),
    ]
    for copy in outs + stores:
        copy.start()

    for copy in mates:
        copy.wait_recv()
    for pack in range(2):
        for array in range(2):
            remote(
                (gk_send, gv_send)[array].at[pack], (gk_in, gv_in)[array].at[pack],
                g_send.at[pack, array], g_recv.at[pack, array], mate,
            ).wait_recv()
    mine = pl.ds(core, 1)
    other = pl.ds(peer, 1)
    gk_fin[mine] = ((gk_mine[mine] + gk_in[mine].astype(jnp.float32)) * scale).astype(jnp.bfloat16)
    gv_fin[mine] = (gv_mine[mine] + gv_in[mine].astype(jnp.float32)).astype(jnp.bfloat16)
    gk_fin[other] = (
        (gk_mate[...][None] + gk_in[other].astype(jnp.float32)) * scale
    ).astype(jnp.bfloat16)
    gv_fin[other] = (gv_mate[...][None] + gv_in[other].astype(jnp.float32)).astype(jnp.bfloat16)
    fins = [
        pltpu.make_async_copy(gk_fin, gk_hbm, fin_sem.at[0]),
        pltpu.make_async_copy(gv_fin, gv_hbm, fin_sem.at[1]),
    ]
    for copy in fins:
        copy.start()

    for copy in kv_out + mate_out + back + mates + outs:
        copy.wait_send()
    for copy in (
        remote(out_buf.at[core], out_hbm.at[peer], o_send.at[0], o_recv.at[0], mate),
        remote(gq_buf.at[core], gq_hbm.at[peer], o_send.at[1], o_recv.at[1], mate),
    ):
        copy.wait_recv()
    for copy in stores + fins:
        copy.wait()


def per_device(queries, keys, values, upstream, doc_ids):
    packs, tok, features = queries.shape
    heads = features // HEAD
    bf16, f32 = jnp.bfloat16, jnp.float32
    wide = heads * tok
    dma = pltpu.SemaphoreType.DMA
    anywhere = pl.BlockSpec(memory_space=pltpu.HBM)
    return pl.pallas_call(
        kernel,
        out_shape=(
            jax.ShapeDtypeStruct(queries.shape, bf16),
            jax.ShapeDtypeStruct(queries.shape, bf16),
            jax.ShapeDtypeStruct(keys.shape, bf16),
            jax.ShapeDtypeStruct(keys.shape, bf16),
        ),
        in_specs=[anywhere] * 5,
        out_specs=(anywhere,) * 4,
        scratch_shapes=[
            pltpu.VMEM((2, tok, features), bf16),
            pltpu.VMEM((2, tok, features), bf16),
            pltpu.VMEM((4, tok, HEAD), bf16),
            pltpu.VMEM((4, tok, HEAD), bf16),
            pltpu.VMEM((2, 4 * tok), jnp.int32),
            pltpu.VMEM((2, 3 * tok, tok), f32),
            pltpu.VMEM((2, 2 * tok, wide), f32),
            pltpu.VMEM((2, 2 * tok, wide), f32),
            pltpu.VMEM((2, 3 * tok, wide), bf16),
            pltpu.VMEM((2, 3 * tok, wide), bf16),
            pltpu.VMEM((2, tok, HEAD), bf16),
            pltpu.VMEM((2, tok, HEAD), bf16),
            pltpu.VMEM((2, tok, HEAD), bf16),
            pltpu.VMEM((2, tok, HEAD), bf16),
            pltpu.VMEM((tok, HEAD), f32),
            pltpu.VMEM((tok, HEAD), f32),
            pltpu.VMEM((2, tok, HEAD), f32),
            pltpu.VMEM((2, tok, HEAD), f32),
            pltpu.VMEM((2, tok, HEAD), bf16),
            pltpu.VMEM((2, tok, HEAD), bf16),
            pltpu.VMEM((2, tok, features), bf16),
            pltpu.VMEM((2, tok, features), bf16),
            dma((4,)),
            dma((2,)),
            dma((2, 2)),
            dma((2, 2)),
            dma((4,)),
            dma((4,)),
            dma((2, 2)),
            dma((2, 2)),
            dma((2,)),
            dma((2,)),
            dma((2,)),
            dma((2,)),
            dma((2,)),
            dma((2,)),
        ],
        compiler_params=pltpu.CompilerParams(
            collective_id=0, has_side_effects=True, vmem_limit_bytes=62 * 1024 * 1024
        ),
        name="attention_both_ways",
    )(queries, keys, values, upstream, doc_ids)


def solution(mesh):
    return jax.shard_map(
        per_device,
        mesh=mesh,
        in_specs=(P("dp", "ctx", None),) * 4 + (P("dp", None),),
        out_specs=(P("dp", "ctx", None),) * 4,
        check_vma=False,
    )
```

time: 190 us -> 21.4 us (0.11)
  the two profiles are of different devices: /device:TPU:2 before, /device:TPU:1 now
where the time goes in v1:
time: 21.4 us; the launch traced here: 21.1 us
  Pallas kernels  16.4 us (77%)
  local copies, waits for them, and re-layouts  4.07 us (19%)
  between operations  0.65 us (3%)
    pallas_call x1, Pallas kernels, per_device(): pl.pallas_call(kernel, out_shape=(jax.ShapeDtypeStruct(queries.shape, bf1...  16.4 us
    unnamed x10, local copies, waits for them, and re-layouts  4.07 us

profile of v1, /device:TPU:1, one launch (start us, length us, event | category | flops | bytes accessed | tf_op | source)
XLA Modules:
  0.0 21.1 jit_solution(13275480277734739162)
XLA Ops:
  0.6 16.4 %attention_both_ways.1 = (bf16[2,128,512]{2,1,0:T(8,128)(2,1)}, bf16[2,128,512]{2,1,0:T(8,128)(2,1)}, bf16[2,128,128]{2,1,0:T(8,128)(2,1)}, bf16[2,128,128]{2,1,0:T(8,128)(2,1)}) custom-call(bf16[2,128,512]{2,1,0:T(8,128)(2,1)} %q_hbm.1, bf16[2,128,128]{2,1,0:T(8,128)(2,1)} %k_hbm.1, bf16[2,128,128]{2,1,0:T(8,128)(2,1)} %v_hbm.1, ...), custom_call_target="tpu_custom_call" | custom-call | tf_op jit(solution)/shard_map/attention_both_ways/pallas_call | solution.py:281
  17.1 0.0 copy-start
  17.1 1.7 %copy.13 = bf16[2,128,512]{2,1,0:T(8,128)(2,1)} copy(bf16[2,128,512]{2,1,0:T(8,128)(2,1)} %get-tuple-element.8) | data formatting | bytes 524288
  18.8 0.0 copy-done
  18.8 0.0 copy-start.2
  18.8 0.7 %copy.14 = bf16[2,128,512]{2,1,0:T(8,128)(2,1)} copy(bf16[2,128,512]{2,1,0:T(8,128)(2,1)S(1)} %copy-done) | data formatting | bytes 524288
  19.5 0.2 copy-done.2
  19.7 0.0 copy-start.1
  19.7 0.6 %copy.15 = bf16[2,128,128]{2,1,0:T(8,128)(2,1)} copy(bf16[2,128,128]{2,1,0:T(8,128)(2,1)S(1)} %copy-done.2) | data formatting | bytes 131072
  20.3 0.2 %copy-done.1 = bf16[2,128,128]{2,1,0:T(8,128)(2,1)S(1)} copy-done((bf16[2,128,128]{2,1,0:T(8,128)(2,1)S(1)}, bf16[2,128,128]{2,1,0:T(8,128)(2,1)}, u32[]{:S(2)}) %copy-start.1) | copy-done | bytes 65560
  20.5 0.6 %copy.16 = bf16[2,128,128]{2,1,0:T(8,128)(2,1)} copy(bf16[2,128,128]{2,1,0:T(8,128)(2,1)S(1)} %copy-done.1) | data formatting | bytes 131072
Async XLA Ops:
  17.1 1.7 %copy-start = (bf16[2,128,512]{2,1,0:T(8,128)(2,1)S(1)}, bf16[2,128,512]{2,1,0:T(8,128)(2,1)}, u32[]{:S(2)}) copy-start(bf16[2,128,512]{2,1,0:T(8,128)(2,1)} %get-tuple-element.9) | copy-start | bytes 786436
  18.8 0.9 %copy-start.2 = (bf16[2,128,128]{2,1,0:T(8,128)(2,1)S(1)}, bf16[2,128,128]{2,1,0:T(8,128)(2,1)}, u32[]{:S(2)}) copy-start(bf16[2,128,128]{2,1,0:T(8,128)(2,1)} %get-tuple-element.10) | copy-start | bytes 196612
  19.7 0.9 %copy-start.1 = (bf16[2,128,128]{2,1,0:T(8,128)(2,1)S(1)}, bf16[2,128,128]{2,1,0:T(8,128)(2,1)}, u32[]{:S(2)}) copy-start(bf16[2,128,128]{2,1,0:T(8,128)(2,1)} %get-tuple-element.11) | copy-start | bytes 196612

commit v2 on v1

v2 whole, which is shorter than its diff:
```python
import math

import jax
import jax.numpy as jnp
from jax import lax
from jax.experimental import pallas as pl
from jax.experimental.pallas import tpu as pltpu
from jax.sharding import PartitionSpec as P

MESH = pl.DeviceIdType.MESH
NEG_LARGE = -1e30
HEAD = 128


def nt(a, b):
    return lax.dot_general(a, b, (((1,), (1,)), ((), ())), preferred_element_type=jnp.float32)


def nn(a, b):
    return lax.dot_general(a, b, (((1,), (0,)), ((), ())), preferred_element_type=jnp.float32)


def stacked(ref, block, heads):
    return jnp.concatenate(
        [ref[block, :, h * HEAD : (h + 1) * HEAD] for h in range(heads)], axis=0
    )


def kernel(
    q_hbm, k_hbm, v_hbm, u_hbm, ids_hbm,
    out_fin, gq_fin, gk_fin, gv_fin,
    q_all, u_all, kv_all, kv_own, ids_v, bias,
    e_loc, d_loc, p_low, s_low,
    g_back, g_in, g_mine, g_mate, out_buf, gq_buf,
    load_sem, kv_send, kv_recv, mate_send, mate_recv,
    g_send, g_recv, gm_send, gm_recv, o_send, o_recv, store_sem,
):
    tok = q_all.shape[1]
    heads = q_all.shape[2] // HEAD
    scale = HEAD**-0.5
    log2_scale = scale * math.log2(math.e)
    ctx = lax.axis_index("ctx")
    dp = lax.axis_index("dp")
    chips = lax.axis_size("ctx") // 2
    chip = ctx // 2
    core = ctx % 2
    peer = 1 - core
    mate = chip * 2 + peer
    has_later = chip < chips - 1
    has_earlier = chip > 0
    later = lax.rem(chip + 1, chips)
    earlier = lax.rem(chip + chips - 1, chips)

    def remote(src, dst, send, recv, target):
        return pltpu.make_async_remote_copy(
            src_ref=src, dst_ref=dst, send_sem=send, recv_sem=recv,
            device_id=(dp, target), device_id_type=MESH,
        )

    barrier = pltpu.get_barrier_semaphore()

    @pl.when(has_earlier)
    def _():
        for target in (earlier * 2, earlier * 2 + 1):
            pl.semaphore_signal(barrier, inc=1, device_id=(dp, target), device_id_type=MESH)

    pl.semaphore_signal(barrier, inc=1, device_id=(dp, mate), device_id_type=MESH)

    ids_first = pl.multiple_of(earlier * 2 * tok, 2 * tok)
    ids_own = pl.multiple_of(chip * 2 * tok, 2 * tok)
    pairs = [
        (k_hbm, kv_own.at[:, 0]),
        (v_hbm, kv_own.at[:, 1]),
        (ids_hbm.at[:, pl.ds(ids_first, 2 * tok)], ids_v.at[:, pl.ds(0, 2 * tok)]),
        (ids_hbm.at[:, pl.ds(ids_own, 2 * tok)], ids_v.at[:, pl.ds(2 * tok, 2 * tok)]),
        (q_hbm.at[core], q_all.at[core]),
        (u_hbm.at[core], u_all.at[core]),
        (k_hbm.at[core], kv_all.at[2 + core, 0]),
        (v_hbm.at[core], kv_all.at[2 + core, 1]),
    ]
    loads = [
        pltpu.make_async_copy(src, dst, load_sem.at[i]) for i, (src, dst) in enumerate(pairs)
    ]
    for copy in loads:
        copy.start()

    @pl.when(jnp.logical_not(has_earlier))
    def _():
        kv_all[0:2] = jnp.zeros((2,) + kv_all.shape[1:], kv_all.dtype)

    @pl.when(jnp.logical_not(has_later))
    def _():
        g_in[...] = jnp.zeros(g_in.shape, g_in.dtype)

    for copy in loads[:2]:
        copy.wait()
    pl.semaphore_wait(barrier, jnp.where(has_later, 3, 1))

    kv_out = [
        remote(kv_own.at[pack], kv_all.at[core], kv_send.at[pack], kv_recv.at[core], later * 2 + pack)
        for pack in range(2)
    ]

    @pl.when(has_later)
    def _():
        for copy in kv_out:
            copy.start()

    def mates(block_pack, place):
        return [
            remote(
                kv_own.at[block_pack], kv_all.at[2 + place], mate_send.at[0], mate_recv.at[0], mate
            ),
            remote(q_hbm.at[block_pack], q_all.at[place], mate_send.at[1], mate_recv.at[1], mate),
            remote(u_hbm.at[block_pack], u_all.at[place], mate_send.at[2], mate_recv.at[2], mate),
        ]

    mate_out = mates(peer, core)
    for copy in mate_out:
        copy.start()

    for copy in loads[2:4]:
        copy.wait()
    ids_two = ids_v[...]
    ids_row = jnp.where(core == 0, ids_two[0:1], ids_two[1:2])
    lane = lax.broadcasted_iota(jnp.int32, ids_row.shape, 1)
    ids_row = jnp.where((lane < 2 * tok) & (chip == 0), -1, ids_row)
    ids_col = jnp.transpose(jnp.broadcast_to(ids_row, (tok, 4 * tok)))
    for block in range(2):
        first = block * tok
        q_first = (2 + block) * tok
        key_pos = first + lax.broadcasted_iota(jnp.int32, (3 * tok, tok), 0)
        query_pos = q_first + lax.broadcasted_iota(jnp.int32, (3 * tok, tok), 1)
        allowed = (ids_col[first : first + 3 * tok] == ids_row[:, q_first : q_first + tok]) & (
            key_pos <= query_pos
        )
        bias[block] = jnp.where(allowed, 0.0, NEG_LARGE)

    for copy in loads[4:]:
        copy.wait()
    for copy in mates(core, peer):
        copy.wait_recv()

    def tile(block, key_first, key_blocks):
        span = key_blocks * tok
        keys = kv_all[key_first : key_first + key_blocks, 0].reshape(span, HEAD)
        vals = kv_all[key_first : key_first + key_blocks, 1].reshape(span, HEAD)
        row = (key_first - block) * tok
        add = bias[block, row : row + span]
        scores = nt(keys, stacked(q_all, block, heads))
        slopes = nt(vals, stacked(u_all, block, heads))
        scores = scores * log2_scale + jnp.concatenate([add] * heads, axis=1)
        return scores, slopes

    local = []
    for block in range(2):
        span = (block + 1) * tok
        scores, slopes = tile(block, 2, block + 1)
        peak = jnp.max(scores, axis=0, keepdims=True)
        weights = jnp.exp2(scores - peak)
        e_loc[block, :span] = weights
        d_loc[block, :span] = slopes
        total = jnp.sum(weights, axis=0, keepdims=True)
        weighted = jnp.sum(weights * slopes, axis=0, keepdims=True)
        local.append((peak, total, weighted))

    @pl.when(has_earlier)
    def _():
        for block in range(2):
            remote(
                kv_own.at[0], kv_all.at[block], kv_send.at[0], kv_recv.at[block], mate
            ).wait_recv()

    stats = []
    back = []
    carry_k = carry_v = None
    for block in range(2):
        span = (2 - block) * tok
        scores, slopes = tile(block, block, 2 - block)
        peak, total, weighted = local[block]
        new_peak = jnp.maximum(peak, jnp.max(scores, axis=0, keepdims=True))
        factor = jnp.exp2(peak - new_peak)
        weights = jnp.exp2(scores - new_peak)
        total = total * factor + jnp.sum(weights, axis=0, keepdims=True)
        weighted = weighted * factor + jnp.sum(weights * slopes, axis=0, keepdims=True)
        inverse = 1.0 / total
        delta = weighted * inverse
        stats.append((factor * inverse, delta))
        prob = weights * inverse
        prob_b = prob.astype(jnp.bfloat16)
        slope_b = (prob * (slopes - delta)).astype(jnp.bfloat16)
        p_low[block, :span] = prob_b
        s_low[block, :span] = slope_b
        part_v = nn(prob_b, stacked(u_all, block, heads))
        part_k = nn(slope_b, stacked(q_all, block, heads))
        if block == 0:
            carry_k, carry_v = part_k[tok:], part_v[tok:]
            done_k, done_v = part_k[:tok], part_v[:tok]
        else:
            done_k, done_v = carry_k + part_k, carry_v + part_v
        g_back[block, 0] = done_k.astype(jnp.bfloat16)
        g_back[block, 1] = done_v.astype(jnp.bfloat16)
        copy = remote(
            g_back.at[block], g_in.at[core], g_send.at[block], g_recv.at[core], earlier * 2 + block
        )
        back.append(copy)
        pl.when(has_earlier)(copy.start)

    for block in range(2):
        span = (block + 1) * tok
        row = (2 - block) * tok
        scaled, delta = stats[block]
        prob = e_loc[block, :span] * scaled
        prob_b = prob.astype(jnp.bfloat16)
        slope_b = (prob * (d_loc[block, :span] - delta)).astype(jnp.bfloat16)
        p_low[block, row:] = prob_b
        s_low[block, row:] = slope_b
        part_v = nn(prob_b, stacked(u_all, block, heads))
        part_k = nn(slope_b, stacked(q_all, block, heads))
        if block == 0:
            carry_k, carry_v = part_k, part_v
        else:
            g_mine[0, 0] = carry_k + part_k[:tok]
            g_mine[0, 1] = carry_v + part_v[:tok]
            g_mine[1, 0] = part_k[tok:]
            g_mine[1, 1] = part_v[tok:]
    swap = remote(g_mine.at[peer], g_mate, gm_send, gm_recv, mate)
    swap.start()

    for block in range(2):
        keys = kv_all[block : block + 3, 0].reshape(3 * tok, HEAD)
        vals = kv_all[block : block + 3, 1].reshape(3 * tok, HEAD)
        out_t = nn(jnp.transpose(vals), p_low[block]).astype(jnp.bfloat16)
        gq_t = (nn(jnp.transpose(keys), s_low[block]) * scale).astype(jnp.bfloat16)
        for h in range(heads):
            cols = slice(h * HEAD, (h + 1) * HEAD)
            rows = slice(h * tok, (h + 1) * tok)
            out_buf[block, :, cols] = jnp.transpose(out_t[:, rows])
            gq_buf[block, :, cols] = jnp.transpose(gq_t[:, rows])
    outs = [
        remote(out_buf.at[peer], out_fin.at[core], o_send.at[0], o_recv.at[0], mate),
        remote(gq_buf.at[peer], gq_fin.at[core], o_send.at[1], o_recv.at[1], mate),
    ]
    stores = [
        pltpu.make_async_copy(out_buf.at[core], out_fin.at[core], store_sem.at[0]),
        pltpu.make_async_copy(gq_buf.at[core], gq_fin.at[core], store_sem.at[1]),
    ]
    for copy in outs + stores:
        copy.start()

    swap.wait_recv()
    for copy in (
        remote(out_buf.at[core], out_fin.at[peer], o_send.at[0], o_recv.at[0], mate),
        remote(gq_buf.at[core], gq_fin.at[peer], o_send.at[1], o_recv.at[1], mate),
    ):
        copy.wait_recv()
    for copy in stores:
        copy.wait()
    for copy in mate_out + outs + [swap]:
        copy.wait_send()

    @pl.when(has_later)
    def _():
        for copy in kv_out:
            copy.wait_send()

    @pl.when(has_earlier)
    def _():
        for copy in back:
            copy.wait_send()

    @pl.when(has_later)
    def _():
        for pack in range(2):
            remote(
                g_back.at[pack], g_in.at[pack], g_send.at[pack], g_recv.at[pack], mate
            ).wait_recv()

    mine = g_mine[pl.ds(core, 1)][0]
    for pack in range(2):
        own = core == pack
        sum_k = jnp.where(own, mine[0], g_mate[0]) + g_in[pack, 0].astype(jnp.float32)
        sum_v = jnp.where(own, mine[1], g_mate[1]) + g_in[pack, 1].astype(jnp.float32)
        gk_fin[pack] = (sum_k * scale).astype(jnp.bfloat16)
        gv_fin[pack] = sum_v.astype(jnp.bfloat16)


def store(*refs):
    count = (len(refs) - 1) // 2
    copies = [
        pltpu.make_async_copy(refs[i], refs[count + i], refs[-1].at[i]) for i in range(count)
    ]
    for copy in copies:
        copy.start()
    for copy in copies:
        copy.wait()


def per_device(queries, keys, values, upstream, doc_ids):
    packs, tok, features = queries.shape
    heads = features // HEAD
    bf16, f32 = jnp.bfloat16, jnp.float32
    wide = heads * tok
    dma = pltpu.SemaphoreType.DMA
    anywhere = pl.BlockSpec(memory_space=pl.ANY)
    shapes = (queries.shape, queries.shape, keys.shape, keys.shape)
    results = pl.pallas_call(
        kernel,
        out_shape=tuple(pltpu.VMEM(shape, bf16) for shape in shapes),
        in_specs=[anywhere] * 5,
        out_specs=(pl.BlockSpec(memory_space=pltpu.VMEM),) * 4,
        scratch_shapes=[
            pltpu.VMEM((2, tok, features), bf16),
            pltpu.VMEM((2, tok, features), bf16),
            pltpu.VMEM((4, 2, tok, HEAD), bf16),
            pltpu.VMEM((2, 2, tok, HEAD), bf16),
            pltpu.VMEM((2, 4 * tok), jnp.int32),
            pltpu.VMEM((2, 3 * tok, tok), f32),
            pltpu.VMEM((2, 2 * tok, wide), f32),
            pltpu.VMEM((2, 2 * tok, wide), f32),
            pltpu.VMEM((2, 3 * tok, wide), bf16),
            pltpu.VMEM((2, 3 * tok, wide), bf16),
            pltpu.VMEM((2, 2, tok, HEAD), bf16),
            pltpu.VMEM((2, 2, tok, HEAD), bf16),
            pltpu.VMEM((2, 2, tok, HEAD), f32),
            pltpu.VMEM((2, tok, HEAD), f32),
            pltpu.VMEM((2, tok, features), bf16),
            pltpu.VMEM((2, tok, features), bf16),
            dma((8,)),
            dma((2,)),
            dma((2,)),
            dma((3,)),
            dma((3,)),
            dma((2,)),
            dma((2,)),
            dma(()),
            dma(()),
            dma((2,)),
            dma((2,)),
            dma((2,)),
        ],
        compiler_params=pltpu.CompilerParams(
            collective_id=0, has_side_effects=True, vmem_limit_bytes=60 * 1024 * 1024
        ),
        name="attention_both_ways",
    )(queries, keys, values, upstream, doc_ids)
    return pl.pallas_call(
        store,
        out_shape=tuple(jax.ShapeDtypeStruct(shape, bf16) for shape in shapes),
        in_specs=[anywhere] * 4,
        out_specs=(anywhere,) * 4,
        scratch_shapes=[dma((4,))],
        compiler_params=pltpu.CompilerParams(vmem_limit_bytes=4 * 1024 * 1024),
        name="store_results",
    )(*results)


def solution(mesh):
    return jax.shard_map(
        per_device,
        mesh=mesh,
        in_specs=(P("dp", "ctx", None),) * 4 + (P("dp", None),),
        out_specs=(P("dp", "ctx", None),) * 4,
        check_vma=False,
    )
```

time: 21.4 us -> 15.2 us (0.71)
  the two profiles are of different devices: /device:TPU:1 before, /device:TPU:251 now
where the time goes in v2:
time: 15.2 us; the launch traced here: 15.1 us
  Pallas kernels  14.5 us (95%)
  between operations  0.64 us (4%)
    pallas_call x1, Pallas kernels, per_device(): pl.pallas_call(kernel, out_shape=tuple((pltpu.VMEM(shape, bf16) for shape...  13.6 us
    pallas_call x1, Pallas kernels, per_device(): pl.pallas_call(store, out_shape=tuple((jax.ShapeDtypeStruct(shape, bf16)...  0.86 us

profile of v2, /device:TPU:251, one launch (start us, length us, event | category | flops | bytes accessed | tf_op | source)
XLA Modules:
  0.0 15.1 jit_solution(16605644737673552784)
XLA Ops:
  0.6 13.6 %attention_both_ways.1 = (bf16[2,128,512]{2,1,0:T(8,128)(2,1)S(1)}, bf16[2,128,512]{2,1,0:T(8,128)(2,1)S(1)}, bf16[2,128,128]{2,1,0:T(8,128)(2,1)S(1)}, bf16[2,128,128]{2,1,0:T(8,128)(2,1)S(1)}) custom-call(bf16[2,128,512]{2,1,0:T(8,128)(2,1)} %q_hbm.1, bf16[2,128,128]{2,1,0:T(8,128)(2,1)} %k_hbm.1, bf16[2,128,128]{2,1,0:T(8,128)(2,1)} %v_hbm.1, ...), custom_call_target="tpu_custom_call" | custom-call | tf_op jit(solution)/shard_map/attention_both_ways/pallas_call | solution.py:307
  14.2 0.9 %store_results.1 = (bf16[2,128,512]{2,1,0:T(8,128)(2,1)}, bf16[2,128,512]{2,1,0:T(8,128)(2,1)}, bf16[2,128,128]{2,1,0:T(8,128)(2,1)}, bf16[2,128,128]{2,1,0:T(8,128)(2,1)}) custom-call(bf16[2,128,512]{2,1,0:T(8,128)(2,1)S(1)} %get-tuple-element.8.refs_0_, bf16[2,128,512]{2,1,0:T(8,128)(2,1)S(1)} %get-tuple-element.9.refs_1_, ...), custom_call_target="tpu_custom_call" | custom-call | tf_op jit(solution)/shard_map/store_results/pallas_call | solution.py:347

commit v3 on v2

v3 whole, which is shorter than its diff:
```python
import math

import jax
import jax.numpy as jnp
from jax import lax
from jax.experimental import pallas as pl
from jax.experimental.pallas import tpu as pltpu
from jax.sharding import PartitionSpec as P

MESH = pl.DeviceIdType.MESH
NEG_LARGE = -1e30
HEAD = 128


def nt(a, b):
    return lax.dot_general(a, b, (((1,), (1,)), ((), ())), preferred_element_type=jnp.float32)


def nn(a, b):
    return lax.dot_general(a, b, (((1,), (0,)), ((), ())), preferred_element_type=jnp.float32)


def kernel(
    q_hbm, k_hbm, v_hbm, u_hbm, ids_hbm,
    out_fin, gq_fin, gk_fin, gv_fin,
    q_all, u_all, kv_all, kv_own, ids_v, bias, stats, norms,
    e_loc, d_loc, p_low, s_low,
    g_back, g_in, g_mine, g_mate, out_buf, gq_buf,
    load_sem, kv_send, kv_recv, mate_send, mate_recv, pass_send, pass_recv,
    g_send, g_recv, gm_send, gm_recv, o_send, o_recv, store_sem,
):
    tok = q_all.shape[2]
    heads = q_all.shape[3] // HEAD
    scale = HEAD**-0.5
    log2_scale = scale * math.log2(math.e)
    ctx = lax.axis_index("ctx")
    dp = lax.axis_index("dp")
    chips = lax.axis_size("ctx") // 2
    chip = ctx // 2
    core = ctx % 2
    peer = 1 - core
    mate = chip * 2 + peer
    has_later = chip < chips - 1
    has_earlier = chip > 0
    later = lax.rem(chip + 1, chips)
    earlier = lax.rem(chip + chips - 1, chips)

    def remote(src, dst, send, recv, target):
        return pltpu.make_async_remote_copy(
            src_ref=src, dst_ref=dst, send_sem=send, recv_sem=recv,
            device_id=(dp, target), device_id_type=MESH,
        )

    barrier = pltpu.get_barrier_semaphore()

    @pl.when(has_earlier & (core == 1))
    def _():
        for target in (earlier * 2 + 1, earlier * 2):
            pl.semaphore_signal(barrier, inc=1, device_id=(dp, target), device_id_type=MESH)

    pl.semaphore_signal(barrier, inc=1, device_id=(dp, mate), device_id_type=MESH)

    ids_first = pl.multiple_of(earlier * 2 * tok, 2 * tok)
    ids_own = pl.multiple_of(chip * 2 * tok, 2 * tok)
    pairs = [
        (k_hbm, kv_own.at[:, 0]),
        (v_hbm, kv_own.at[:, 1]),
        (ids_hbm.at[:, pl.ds(ids_first, 2 * tok)], ids_v.at[:, pl.ds(0, 2 * tok)]),
        (ids_hbm.at[:, pl.ds(ids_own, 2 * tok)], ids_v.at[:, pl.ds(2 * tok, 2 * tok)]),
        (q_hbm, q_all.at[:, core]),
        (u_hbm, u_all.at[:, core]),
        (k_hbm, kv_all.at[:, 2 + core, 0]),
        (v_hbm, kv_all.at[:, 2 + core, 1]),
    ]
    loads = [
        pltpu.make_async_copy(src, dst, load_sem.at[i]) for i, (src, dst) in enumerate(pairs)
    ]
    for copy in loads:
        copy.start()

    @pl.when(jnp.logical_not(has_earlier))
    def _():
        for pack in range(2):
            kv_all[pack, 0:2] = jnp.zeros((2,) + kv_all.shape[2:], kv_all.dtype)

    @pl.when(jnp.logical_not(has_later))
    def _():
        g_in[...] = jnp.zeros(g_in.shape, g_in.dtype)

    for copy in loads[:2]:
        copy.wait()
    pl.semaphore_wait(barrier, jnp.where(has_later, 2, 1))

    kv_out = [
        remote(
            kv_own.at[pack], kv_all.at[pack, core], kv_send.at[pack], kv_recv.at[pack, core],
            later * 2 + 1,
        )
        for pack in range(2)
    ]

    @pl.when(has_later)
    def _():
        for copy in kv_out:
            copy.start()

    def mates(pack, block):
        return [
            remote(src.at[pack], dst, mate_send.at[pack, i], mate_recv.at[pack, i], mate)
            for i, (src, dst) in enumerate(
                (
                    (kv_own, kv_all.at[pack, 2 + block]),
                    (q_hbm, q_all.at[pack, block]),
                    (u_hbm, u_all.at[pack, block]),
                )
            )
        ]

    mate_out = [mates(0, core), mates(1, 0)]
    for copy in mate_out[0]:
        copy.start()

    @pl.when(core == 0)
    def _():
        for copy in mate_out[1]:
            copy.start()

    for copy in loads[2:4]:
        copy.wait()
    ids_two = ids_v[...]
    for pack in range(2):
        ids_row = ids_two[pack : pack + 1]
        lane = lax.broadcasted_iota(jnp.int32, ids_row.shape, 1)
        ids_row = jnp.where((lane < 2 * tok) & (chip == 0), -1, ids_row)
        ids_col = jnp.transpose(jnp.broadcast_to(ids_row, (tok, 4 * tok)))
        for block in range(2):
            first = block * tok
            q_first = (2 + block) * tok
            key_pos = first + lax.broadcasted_iota(jnp.int32, (3 * tok, tok), 0)
            query_pos = q_first + lax.broadcasted_iota(jnp.int32, (3 * tok, tok), 1)
            allowed = (ids_col[first : first + 3 * tok] == ids_row[:, q_first : q_first + tok]) & (
                key_pos <= query_pos
            )
            bias[pack, block] = jnp.where(allowed, 0.0, NEG_LARGE)

    def stacked(ref, pack, block):
        return jnp.concatenate(
            [ref[pack, block, :, h * HEAD : (h + 1) * HEAD] for h in range(heads)], axis=0
        )

    def tile(pack, block, key_first, key_blocks):
        span = key_blocks * tok
        keys = kv_all[pack, key_first : key_first + key_blocks, 0].reshape(span, HEAD)
        vals = kv_all[pack, key_first : key_first + key_blocks, 1].reshape(span, HEAD)
        row = (key_first - block) * tok
        add = bias[pack, block, row : row + span]
        scores = nt(keys, stacked(q_all, pack, block))
        slopes = nt(vals, stacked(u_all, pack, block))
        scores = scores * log2_scale + jnp.concatenate([add] * heads, axis=1)
        return scores, slopes

    def local_part(pack, keep):
        for block in range(2):
            span = (block + 1) * tok
            scores, slopes = tile(pack, block, 2, block + 1)
            peak = jnp.max(scores, axis=0, keepdims=True)
            weights = jnp.exp2(scores - peak)
            if keep:
                e_loc[block, :span] = weights
                d_loc[block, :span] = slopes
            stats[pack, block, 0:1] = peak
            stats[pack, block, 1:2] = jnp.sum(weights, axis=0, keepdims=True)
            stats[pack, block, 2:3] = jnp.sum(weights * slopes, axis=0, keepdims=True)

    def back_copy(pack, block):
        return remote(
            g_back.at[pack, block], g_in.at[pack], g_send.at[pack, block], g_recv.at[pack],
            earlier * 2 + block,
        )

    def boundary_part(pack, keep, send):
        for block in range(2):
            span = (2 - block) * tok
            scores, slopes = tile(pack, block, block, 2 - block)
            peak = stats[pack, block, 0:1]
            new_peak = jnp.maximum(peak, jnp.max(scores, axis=0, keepdims=True))
            factor = jnp.exp2(peak - new_peak)
            weights = jnp.exp2(scores - new_peak)
            total = stats[pack, block, 1:2] * factor + jnp.sum(weights, axis=0, keepdims=True)
            weighted = stats[pack, block, 2:3] * factor + jnp.sum(
                weights * slopes, axis=0, keepdims=True
            )
            inverse = 1.0 / total
            delta = weighted * inverse
            prob = weights * inverse
            prob_b = prob.astype(jnp.bfloat16)
            slope_b = (prob * (slopes - delta)).astype(jnp.bfloat16)
            if keep:
                norms[block, 0:1] = factor * inverse
                norms[block, 1:2] = delta
                p_low[block, :span] = prob_b
                s_low[block, :span] = slope_b
            if send:
                part_v = nn(prob_b, stacked(u_all, pack, block))
                part_k = nn(slope_b, stacked(q_all, pack, block))
                if block == 0:
                    carry_k, carry_v = part_k[tok:], part_v[tok:]
                    done_k, done_v = part_k[:tok], part_v[:tok]
                else:
                    done_k, done_v = carry_k + part_k, carry_v + part_v
                g_back[pack, block, 0] = done_k.astype(jnp.bfloat16)
                g_back[pack, block, 1] = done_v.astype(jnp.bfloat16)
                pl.when(has_earlier)(back_copy(pack, block).start)

    def kv_in(pack):
        for block in range(2):
            remote(
                kv_own.at[0], kv_all.at[pack, block], kv_send.at[0], kv_recv.at[pack, block], mate
            ).wait_recv()

    passed = remote(kv_all.at[0, pl.ds(0, 2)], kv_all.at[0, pl.ds(0, 2)], pass_send, pass_recv, mate)

    for copy in loads[4:]:
        copy.wait()
    for copy in mates(0, peer):
        copy.wait_recv()

    @pl.when(core == 0)
    def _():
        local_part(0, True)
        pl.when(has_earlier)(passed.wait_recv)
        boundary_part(0, True, False)

    @pl.when(core == 1)
    def _():
        local_part(0, False)
        for copy in mates(1, 0):
            copy.wait_recv()
        local_part(1, True)

        @pl.when(has_earlier)
        def _():
            kv_in(0)
            passed.start()

        boundary_part(0, False, True)

        @pl.when(has_earlier)
        def _():
            kv_in(1)

        boundary_part(1, True, True)

    for block in range(2):
        span = (block + 1) * tok
        row = (2 - block) * tok
        prob = e_loc[block, :span] * norms[block, 0:1]
        prob_b = prob.astype(jnp.bfloat16)
        slope_b = (prob * (d_loc[block, :span] - norms[block, 1:2])).astype(jnp.bfloat16)
        p_low[block, row:] = prob_b
        s_low[block, row:] = slope_b
        part_v = nn(prob_b, stacked(u_all, core, block))
        part_k = nn(slope_b, stacked(q_all, core, block))
        if block == 0:
            carry_k, carry_v = part_k, part_v
        else:
            g_mine[0, 0] = carry_k + part_k[:tok]
            g_mine[0, 1] = carry_v + part_v[:tok]
            g_mine[1, 0] = part_k[tok:]
            g_mine[1, 1] = part_v[tok:]
    swap = remote(g_mine.at[peer], g_mate, gm_send, gm_recv, mate)
    swap.start()

    for block in range(2):
        keys = kv_all[core, block : block + 3, 0].reshape(3 * tok, HEAD)
        vals = kv_all[core, block : block + 3, 1].reshape(3 * tok, HEAD)
        out_t = nn(jnp.transpose(vals), p_low[block]).astype(jnp.bfloat16)
        gq_t = (nn(jnp.transpose(keys), s_low[block]) * scale).astype(jnp.bfloat16)
        for h in range(heads):
            cols = slice(h * HEAD, (h + 1) * HEAD)
            rows = slice(h * tok, (h + 1) * tok)
            out_buf[block, :, cols] = jnp.transpose(out_t[:, rows])
            gq_buf[block, :, cols] = jnp.transpose(gq_t[:, rows])
    outs = [
        remote(out_buf.at[peer], out_fin.at[core], o_send.at[0], o_recv.at[0], mate),
        remote(gq_buf.at[peer], gq_fin.at[core], o_send.at[1], o_recv.at[1], mate),
    ]
    stores = [
        pltpu.make_async_copy(out_buf.at[core], out_fin.at[core], store_sem.at[0]),
        pltpu.make_async_copy(gq_buf.at[core], gq_fin.at[core], store_sem.at[1]),
    ]
    for copy in outs + stores:
        copy.start()

    swap.wait_recv()
    for copy in (
        remote(out_buf.at[core], out_fin.at[peer], o_send.at[0], o_recv.at[0], mate),
        remote(gq_buf.at[core], gq_fin.at[peer], o_send.at[1], o_recv.at[1], mate),
    ):
        copy.wait_recv()
    for copy in stores:
        copy.wait()
    for copy in mate_out[0] + outs + [swap]:
        copy.wait_send()

    @pl.when(core == 0)
    def _():
        for copy in mate_out[1]:
            copy.wait_send()

    @pl.when(has_later)
    def _():
        for copy in kv_out:
            copy.wait_send()

    @pl.when(has_earlier & (core == 1))
    def _():
        passed.wait_send()
        for pack in range(2):
            for block in range(2):
                back_copy(pack, block).wait_send()

    @pl.when(has_later)
    def _():
        for pack in range(2):
            remote(
                g_back.at[pack, 0], g_in.at[pack], g_send.at[pack, 0], g_recv.at[pack], mate
            ).wait_recv()

    mine = g_mine[pl.ds(core, 1)][0]
    for pack in range(2):
        own = core == pack
        sum_k = jnp.where(own, mine[0], g_mate[0]) + g_in[pack, 0].astype(jnp.float32)
        sum_v = jnp.where(own, mine[1], g_mate[1]) + g_in[pack, 1].astype(jnp.float32)
        gk_fin[pack] = (sum_k * scale).astype(jnp.bfloat16)
        gv_fin[pack] = sum_v.astype(jnp.bfloat16)


def store(*refs):
    count = (len(refs) - 1) // 2
    copies = [
        pltpu.make_async_copy(refs[i], refs[count + i], refs[-1].at[i]) for i in range(count)
    ]
    for copy in copies:
        copy.start()
    for copy in copies:
        copy.wait()


def per_device(queries, keys, values, upstream, doc_ids):
    packs, tok, features = queries.shape
    heads = features // HEAD
    bf16, f32 = jnp.bfloat16, jnp.float32
    wide = heads * tok
    dma = pltpu.SemaphoreType.DMA
    anywhere = pl.BlockSpec(memory_space=pl.ANY)
    shapes = (queries.shape, queries.shape, keys.shape, keys.shape)
    results = pl.pallas_call(
        kernel,
        out_shape=tuple(pltpu.VMEM(shape, bf16) for shape in shapes),
        in_specs=[anywhere] * 5,
        out_specs=(pl.BlockSpec(memory_space=pltpu.VMEM),) * 4,
        scratch_shapes=[
            pltpu.VMEM((2, 2, tok, features), bf16),
            pltpu.VMEM((2, 2, tok, features), bf16),
            pltpu.VMEM((2, 4, 2, tok, HEAD), bf16),
            pltpu.VMEM((2, 2, tok, HEAD), bf16),
            pltpu.VMEM((2, 4 * tok), jnp.int32),
            pltpu.VMEM((2, 2, 3 * tok, tok), f32),
            pltpu.VMEM((2, 2, 8, wide), f32),
            pltpu.VMEM((2, 8, wide), f32),
            pltpu.VMEM((2, 2 * tok, wide), f32),
            pltpu.VMEM((2, 2 * tok, wide), f32),
            pltpu.VMEM((2, 3 * tok, wide), bf16),
            pltpu.VMEM((2, 3 * tok, wide), bf16),
            pltpu.VMEM((2, 2, 2, tok, HEAD), bf16),
            pltpu.VMEM((2, 2, tok, HEAD), bf16),
            pltpu.VMEM((2, 2, tok, HEAD), f32),
            pltpu.VMEM((2, tok, HEAD), f32),
            pltpu.VMEM((2, tok, features), bf16),
            pltpu.VMEM((2, tok, features), bf16),
            dma((8,)),
            dma((2,)),
            dma((2, 2)),
            dma((2, 3)),
            dma((2, 3)),
            dma(()),
            dma(()),
            dma((2, 2)),
            dma((2,)),
            dma(()),
            dma(()),
            dma((2,)),
            dma((2,)),
            dma((2,)),
        ],
        compiler_params=pltpu.CompilerParams(
            collective_id=0, has_side_effects=True, vmem_limit_bytes=60 * 1024 * 1024
        ),
        name="attention_both_ways",
    )(queries, keys, values, upstream, doc_ids)
    return pl.pallas_call(
        store,
        out_shape=tuple(jax.ShapeDtypeStruct(shape, bf16) for shape in shapes),
        in_specs=[anywhere] * 4,
        out_specs=(anywhere,) * 4,
        scratch_shapes=[dma((4,))],
        compiler_params=pltpu.CompilerParams(vmem_limit_bytes=4 * 1024 * 1024),
        name="store_results",
    )(*results)


def solution(mesh):
    return jax.shard_map(
        per_device,
        mesh=mesh,
        in_specs=(P("dp", "ctx", None),) * 4 + (P("dp", None),),
        out_specs=(P("dp", "ctx", None),) * 4,
        check_vma=False,
    )
```

time: 15.2 us -> 14.4 us (0.947)
  the two profiles are of different devices: /device:TPU:251 before, /device:TPU:1 now
where the time goes in v3:
time: 14.4 us; the launch traced here: 14.2 us
  Pallas kernels  13.6 us (94%)
  between operations  0.64 us (4%)
    pallas_call x1, Pallas kernels, per_device(): pl.pallas_call(kernel, out_shape=tuple((pltpu.VMEM(shape, bf16) for shape...  12.7 us
    pallas_call x1, Pallas kernels, per_device(): pl.pallas_call(store, out_shape=tuple((jax.ShapeDtypeStruct(shape, bf16)...  0.86 us

profile of v3, /device:TPU:1, one launch (start us, length us, event | category | flops | bytes accessed | tf_op | source)
XLA Modules:
  0.0 14.2 jit_solution(5332230315474301204)
XLA Ops:
  0.6 12.7 %attention_both_ways.1 = (bf16[2,128,512]{2,1,0:T(8,128)(2,1)S(1)}, bf16[2,128,512]{2,1,0:T(8,128)(2,1)S(1)}, bf16[2,128,128]{2,1,0:T(8,128)(2,1)S(1)}, bf16[2,128,128]{2,1,0:T(8,128)(2,1)S(1)}) custom-call(bf16[2,128,512]{2,1,0:T(8,128)(2,1)} %q_hbm.1, bf16[2,128,128]{2,1,0:T(8,128)(2,1)} %k_hbm.1, bf16[2,128,128]{2,1,0:T(8,128)(2,1)} %v_hbm.1, ...), custom_call_target="tpu_custom_call" | custom-call | tf_op jit(solution)/shard_map/attention_both_ways/pallas_call | solution.py:358
  13.4 0.9 %store_results.1 = (bf16[2,128,512]{2,1,0:T(8,128)(2,1)}, bf16[2,128,512]{2,1,0:T(8,128)(2,1)}, bf16[2,128,128]{2,1,0:T(8,128)(2,1)}, bf16[2,128,128]{2,1,0:T(8,128)(2,1)}) custom-call(bf16[2,128,512]{2,1,0:T(8,128)(2,1)S(1)} %get-tuple-element.8.refs_0_, bf16[2,128,512]{2,1,0:T(8,128)(2,1)S(1)} %get-tuple-element.9.refs_1_, ...), custom_call_target="tpu_custom_call" | custom-call | tf_op jit(solution)/shard_map/store_results/pallas_call | solution.py:402

commit v4 on v3

--- a/solution.py
+++ b/solution.py
@@ -101,8 +101,7 @@
 
     @pl.when(has_later)
     def _():
-        for copy in kv_out:
-            copy.start()
+        kv_out[0].start()
 
     def mates(pack, block):
         return [
@@ -124,6 +123,10 @@
     def _():
         for copy in mate_out[1]:
             copy.start()
+
+    @pl.when(has_later & (core == 0))
+    def _():
+        kv_out[1].start()
 
     for copy in loads[2:4]:
         copy.wait()
@@ -210,7 +213,16 @@
                     done_k, done_v = carry_k + part_k, carry_v + part_v
                 g_back[pack, block, 0] = done_k.astype(jnp.bfloat16)
                 g_back[pack, block, 1] = done_v.astype(jnp.bfloat16)
-                pl.when(has_earlier)(back_copy(pack, block).start)
+                back_copy(pack, block).start()
+
+    def no_boundary(pack):
+        for block in range(2):
+            inverse = 1.0 / stats[pack, block, 1:2]
+            norms[block, 0:1] = inverse
+            norms[block, 1:2] = stats[pack, block, 2:3] * inverse
+            span = (2 - block) * tok
+            p_low[block, :span] = jnp.zeros((span, heads * tok), jnp.bfloat16)
+            s_low[block, :span] = jnp.zeros((span, heads * tok), jnp.bfloat16)
 
     def kv_in(pack):
         for block in range(2):
@@ -225,11 +237,19 @@
     for copy in mates(0, peer):
         copy.wait_recv()
 
+    @pl.when(has_later & (core == 1))
+    def _():
+        kv_out[1].start()
+
+
     @pl.when(core == 0)
     def _():
         local_part(0, True)
-        pl.when(has_earlier)(passed.wait_recv)
-        boundary_part(0, True, False)
+
+        @pl.when(has_earlier)
+        def _():
+            passed.wait_recv()
+            boundary_part(0, True, False)
 
     @pl.when(core == 1)
     def _():
@@ -242,14 +262,13 @@
         def _():
             kv_in(0)
             passed.start()
-
-        boundary_part(0, False, True)
-
-        @pl.when(has_earlier)
-        def _():
+            boundary_part(0, False, True)
             kv_in(1)
-
-        boundary_part(1, True, True)
+            boundary_part(1, True, True)
+
+    @pl.when(jnp.logical_not(has_earlier))
+    def _():
+        no_boundary(core)
 
     for block in range(2):
         span = (block + 1) * tok

time: 14.4 us -> 14 us (0.972)
  Pallas kernels: 13.6 us -> 13.3 us
    pallas_call x1, Pallas kernels: 12.7 us -> 12.4 us  [per_device(): pl.pallas_call(kernel, out_shape=tuple((pltpu.VMEM(shape, bf16) for shape...]
where the time goes in v4:
time: 14 us; the launch traced here: 13.9 us
  Pallas kernels  13.3 us (95%)
  between operations  0.64 us (5%)
    pallas_call x1, Pallas kernels, per_device(): pl.pallas_call(kernel, out_shape=tuple((pltpu.VMEM(shape, bf16) for shape...  12.4 us
    pallas_call x1, Pallas kernels, per_device(): pl.pallas_call(store, out_shape=tuple((jax.ShapeDtypeStruct(shape, bf16)...  0.86 us

profile of v4, /device:TPU:1, one launch (start us, length us, event | category | flops | bytes accessed | tf_op | source)
XLA Modules:
  0.0 13.9 jit_solution(2129050103751590570)
XLA Ops:
  0.6 12.4 %attention_both_ways.1 = (bf16[2,128,512]{2,1,0:T(8,128)(2,1)S(1)}, bf16[2,128,512]{2,1,0:T(8,128)(2,1)S(1)}, bf16[2,128,128]{2,1,0:T(8,128)(2,1)S(1)}, bf16[2,128,128]{2,1,0:T(8,128)(2,1)S(1)}) custom-call(bf16[2,128,512]{2,1,0:T(8,128)(2,1)} %q_hbm.1, bf16[2,128,128]{2,1,0:T(8,128)(2,1)} %k_hbm.1, bf16[2,128,128]{2,1,0:T(8,128)(2,1)} %v_hbm.1, ...), custom_call_target="tpu_custom_call" | custom-call | tf_op jit(solution)/shard_map/attention_both_ways/pallas_call | solution.py:377
  13.0 0.9 %store_results.1 = (bf16[2,128,512]{2,1,0:T(8,128)(2,1)}, bf16[2,128,512]{2,1,0:T(8,128)(2,1)}, bf16[2,128,128]{2,1,0:T(8,128)(2,1)}, bf16[2,128,128]{2,1,0:T(8,128)(2,1)}) custom-call(bf16[2,128,512]{2,1,0:T(8,128)(2,1)S(1)} %get-tuple-element.8.refs_0_, bf16[2,128,512]{2,1,0:T(8,128)(2,1)S(1)} %get-tuple-element.9.refs_1_, ...), custom_call_target="tpu_custom_call" | custom-call | tf_op jit(solution)/shard_map/store_results/pallas_call | solution.py:421

commit v5 on v4

--- a/solution.py
+++ b/solution.py
@@ -63,8 +63,10 @@
     ids_first = pl.multiple_of(earlier * 2 * tok, 2 * tok)
     ids_own = pl.multiple_of(chip * 2 * tok, 2 * tok)
     pairs = [
-        (k_hbm, kv_own.at[:, 0]),
-        (v_hbm, kv_own.at[:, 1]),
+        (k_hbm.at[0], kv_own.at[0, 0]),
+        (v_hbm.at[0], kv_own.at[0, 1]),
+        (k_hbm.at[1], kv_own.at[1, 0]),
+        (v_hbm.at[1], kv_own.at[1, 1]),
         (ids_hbm.at[:, pl.ds(ids_first, 2 * tok)], ids_v.at[:, pl.ds(0, 2 * tok)]),
         (ids_hbm.at[:, pl.ds(ids_own, 2 * tok)], ids_v.at[:, pl.ds(2 * tok, 2 * tok)]),
         (q_hbm, q_all.at[:, core]),
@@ -87,7 +89,7 @@
     def _():
         g_in[...] = jnp.zeros(g_in.shape, g_in.dtype)
 
-    for copy in loads[:2]:
+    for copy in loads[:4]:
         copy.wait()
     pl.semaphore_wait(barrier, jnp.where(has_later, 2, 1))
 
@@ -128,7 +130,7 @@
     def _():
         kv_out[1].start()
 
-    for copy in loads[2:4]:
+    for copy in loads[4:6]:
         copy.wait()
     ids_two = ids_v[...]
     for pack in range(2):
@@ -213,7 +215,11 @@
                     done_k, done_v = carry_k + part_k, carry_v + part_v
                 g_back[pack, block, 0] = done_k.astype(jnp.bfloat16)
                 g_back[pack, block, 1] = done_v.astype(jnp.bfloat16)
-                back_copy(pack, block).start()
+                if block == 0:
+                    pl.when(chip != 1)(back_copy(pack, 0).start)
+                else:
+                    back_copy(pack, 1).start()
+                    pl.when(chip == 1)(back_copy(pack, 0).start)
 
     def no_boundary(pack):
         for block in range(2):
@@ -232,7 +238,7 @@
 
     passed = remote(kv_all.at[0, pl.ds(0, 2)], kv_all.at[0, pl.ds(0, 2)], pass_send, pass_recv, mate)
 
-    for copy in loads[4:]:
+    for copy in loads[6:]:
         copy.wait()
     for copy in mates(0, peer):
         copy.wait_recv()
@@ -339,20 +345,18 @@
             for block in range(2):
                 back_copy(pack, block).wait_send()
 
-    @pl.when(has_later)
-    def _():
-        for pack in range(2):
-            remote(
-                g_back.at[pack, 0], g_in.at[pack], g_send.at[pack, 0], g_recv.at[pack], mate
-            ).wait_recv()
-
     mine = g_mine[pl.ds(core, 1)][0]
     for pack in range(2):
         own = core == pack
-        sum_k = jnp.where(own, mine[0], g_mate[0]) + g_in[pack, 0].astype(jnp.float32)
-        sum_v = jnp.where(own, mine[1], g_mate[1]) + g_in[pack, 1].astype(jnp.float32)
-        gk_fin[pack] = (sum_k * scale).astype(jnp.bfloat16)
-        gv_fin[pack] = sum_v.astype(jnp.bfloat16)
+        sum_k = jnp.where(own, mine[0], g_mate[0])
+        sum_v = jnp.where(own, mine[1], g_mate[1])
+        pl.when(has_later)(
+            remote(
+                g_back.at[pack, 0], g_in.at[pack], g_send.at[pack, 0], g_recv.at[pack], mate
+            ).wait_recv
+        )
+        gk_fin[pack] = ((sum_k + g_in[pack, 0].astype(jnp.float32)) * scale).astype(jnp.bfloat16)
+        gv_fin[pack] = (sum_v + g_in[pack, 1].astype(jnp.float32)).astype(jnp.bfloat16)
 
 
 def store(*refs):
@@ -398,7 +402,7 @@
             pltpu.VMEM((2, tok, HEAD), f32),
             pltpu.VMEM((2, tok, features), bf16),
             pltpu.VMEM((2, tok, features), bf16),
-            dma((8,)),
+            dma((10,)),
             dma((2,)),
             dma((2, 2)),
             dma((2, 3)),

time: 14 us -> 13.7 us (0.979)
  Pallas kernels: 13.3 us -> 13 us
    pallas_call x1, Pallas kernels: 12.4 us -> 12.1 us  [per_device(): pl.pallas_call(kernel, out_shape=tuple((pltpu.VMEM(shape, bf16) for shape...]
where the time goes in v5:
time: 13.7 us; the launch traced here: 13.6 us
  Pallas kernels  13 us (95%)
  between operations  0.64 us (5%)
    pallas_call x1, Pallas kernels, per_device(): pl.pallas_call(kernel, out_shape=tuple((pltpu.VMEM(shape, bf16) for shape...  12.1 us
    pallas_call x1, Pallas kernels, per_device(): pl.pallas_call(store, out_shape=tuple((jax.ShapeDtypeStruct(shape, bf16)...  0.86 us

profile of v5, /device:TPU:1, one launch (start us, length us, event | category | flops | bytes accessed | tf_op | source)
XLA Modules:
  0.0 13.6 jit_solution(11504077982163663869)
XLA Ops:
  0.6 12.1 %attention_both_ways.1 = (bf16[2,128,512]{2,1,0:T(8,128)(2,1)S(1)}, bf16[2,128,512]{2,1,0:T(8,128)(2,1)S(1)}, bf16[2,128,128]{2,1,0:T(8,128)(2,1)S(1)}, bf16[2,128,128]{2,1,0:T(8,128)(2,1)S(1)}) custom-call(bf16[2,128,512]{2,1,0:T(8,128)(2,1)} %q_hbm.1, bf16[2,128,128]{2,1,0:T(8,128)(2,1)} %k_hbm.1, bf16[2,128,128]{2,1,0:T(8,128)(2,1)} %v_hbm.1, ...), custom_call_target="tpu_custom_call" | custom-call | tf_op jit(solution)/shard_map/attention_both_ways/pallas_call | solution.py:381
  12.8 0.9 %store_results.1 = (bf16[2,128,512]{2,1,0:T(8,128)(2,1)}, bf16[2,128,512]{2,1,0:T(8,128)(2,1)}, bf16[2,128,128]{2,1,0:T(8,128)(2,1)}, bf16[2,128,128]{2,1,0:T(8,128)(2,1)}) custom-call(bf16[2,128,512]{2,1,0:T(8,128)(2,1)S(1)} %get-tuple-element.8.refs_0_, bf16[2,128,512]{2,1,0:T(8,128)(2,1)S(1)} %get-tuple-element.9.refs_1_, ...), custom_call_target="tpu_custom_call" | custom-call | tf_op jit(solution)/shard_map/store_results/pallas_call | solution.py:425

commit v6 on v5

--- a/solution.py
+++ b/solution.py
@@ -89,10 +89,6 @@
     def _():
         g_in[...] = jnp.zeros(g_in.shape, g_in.dtype)
 
-    for copy in loads[:4]:
-        copy.wait()
-    pl.semaphore_wait(barrier, jnp.where(has_later, 2, 1))
-
     kv_out = [
         remote(
             kv_own.at[pack], kv_all.at[pack, core], kv_send.at[pack], kv_recv.at[pack, core],
@@ -101,9 +97,24 @@
         for pack in range(2)
     ]
 
-    @pl.when(has_later)
-    def _():
-        kv_out[0].start()
+    @pl.when(core == 0)
+    def _():
+        pl.semaphore_wait(barrier, jnp.where(has_later, 2, 1))
+
+        @pl.when(has_later)
+        def _():
+            for i, src in enumerate((k_hbm, v_hbm)):
+                remote(
+                    src.at[0], kv_all.at[0, 0, i], kv_send.at[0], kv_recv.at[0, 0], later * 2 + 1
+                ).start()
+
+
+    @pl.when(core == 1)
+    def _():
+        for copy in loads[:4]:
+            copy.wait()
+        pl.semaphore_wait(barrier, jnp.where(has_later, 2, 1))
+        pl.when(has_later)(kv_out[0].start)
 
     def mates(pack, block):
         return [
@@ -118,17 +129,21 @@
         ]
 
     mate_out = [mates(0, core), mates(1, 0)]
-    for copy in mate_out[0]:
+    for copy in mate_out[0][1:]:
         copy.start()
 
     @pl.when(core == 0)
     def _():
+        for copy in loads[:4]:
+            copy.wait()
+
+    mate_out[0][0].start()
+
+    @pl.when(core == 0)
+    def _():
+        pl.when(has_later)(kv_out[1].start)
         for copy in mate_out[1]:
             copy.start()
-
-    @pl.when(has_later & (core == 0))
-    def _():
-        kv_out[1].start()
 
     for copy in loads[4:6]:
         copy.wait()

time: 13.7 us -> 13.5 us (0.985)
  Pallas kernels: 13 us -> 12.7 us
    pallas_call x1, Pallas kernels: 12.1 us -> 11.8 us  [per_device(): pl.pallas_call(kernel, out_shape=tuple((pltpu.VMEM(shape, bf16) for shape...]
where the time goes in v6:
time: 13.5 us; the launch traced here: 13.3 us
  Pallas kernels  12.7 us (94%)
  between operations  0.64 us (5%)
    pallas_call x1, Pallas kernels, per_device(): pl.pallas_call(kernel, out_shape=tuple((pltpu.VMEM(shape, bf16) for shape...  11.8 us
    pallas_call x1, Pallas kernels, per_device(): pl.pallas_call(store, out_shape=tuple((jax.ShapeDtypeStruct(shape, bf16)...  0.86 us

profile of v6, /device:TPU:1, one launch (start us, length us, event | category | flops | bytes accessed | tf_op | source)
XLA Modules:
  0.0 13.3 jit_solution(13911155497410434956)
XLA Ops:
  0.6 11.8 %attention_both_ways.1 = (bf16[2,128,512]{2,1,0:T(8,128)(2,1)S(1)}, bf16[2,128,512]{2,1,0:T(8,128)(2,1)S(1)}, bf16[2,128,128]{2,1,0:T(8,128)(2,1)S(1)}, bf16[2,128,128]{2,1,0:T(8,128)(2,1)S(1)}) custom-call(bf16[2,128,512]{2,1,0:T(8,128)(2,1)} %q_hbm.1, bf16[2,128,128]{2,1,0:T(8,128)(2,1)} %k_hbm.1, bf16[2,128,128]{2,1,0:T(8,128)(2,1)} %v_hbm.1, ...), custom_call_target="tpu_custom_call" | custom-call | tf_op jit(solution)/shard_map/attention_both_ways/pallas_call | solution.py:396
  12.5 0.9 %store_results.1 = (bf16[2,128,512]{2,1,0:T(8,128)(2,1)}, bf16[2,128,512]{2,1,0:T(8,128)(2,1)}, bf16[2,128,128]{2,1,0:T(8,128)(2,1)}, bf16[2,128,128]{2,1,0:T(8,128)(2,1)}) custom-call(bf16[2,128,512]{2,1,0:T(8,128)(2,1)S(1)} %get-tuple-element.8.refs_0_, bf16[2,128,512]{2,1,0:T(8,128)(2,1)S(1)} %get-tuple-element.9.refs_1_, ...), custom_call_target="tpu_custom_call" | custom-call | tf_op jit(solution)/shard_map/store_results/pallas_call | solution.py:440

commit v7 on v6

--- a/solution.py
+++ b/solution.py
@@ -77,8 +77,13 @@
     loads = [
         pltpu.make_async_copy(src, dst, load_sem.at[i]) for i, (src, dst) in enumerate(pairs)
     ]
-    for copy in loads:
+    for copy in loads[:4]:
         copy.start()
+
+    @pl.when(core == 1)
+    def _():
+        for copy in loads[4:]:
+            copy.start()
 
     @pl.when(jnp.logical_not(has_earlier))
     def _():
@@ -108,6 +113,8 @@
                     src.at[0], kv_all.at[0, 0, i], kv_send.at[0], kv_recv.at[0, 0], later * 2 + 1
                 ).start()
 
+        for copy in loads[4:]:
+            copy.start()
 
     @pl.when(core == 1)
     def _():

time: 13.5 us -> 13.6 us (level)
  no operation moved by 1% of the time
where the time goes in v7:
time: 13.6 us; the launch traced here: 13.3 us
  Pallas kernels  12.7 us (93%)
  between operations  0.64 us (5%)
    pallas_call x1, Pallas kernels, per_device(): pl.pallas_call(kernel, out_shape=tuple((pltpu.VMEM(shape, bf16) for shape...  11.8 us
    pallas_call x1, Pallas kernels, per_device(): pl.pallas_call(store, out_shape=tuple((jax.ShapeDtypeStruct(shape, bf16)...  0.86 us

profile of v7, /device:TPU:1, one launch (start us, length us, event | category | flops | bytes accessed | tf_op | source)
XLA Modules:
  0.0 13.3 jit_solution(17057919065439831004)
XLA Ops:
  0.6 11.8 %attention_both_ways.1 = (bf16[2,128,512]{2,1,0:T(8,128)(2,1)S(1)}, bf16[2,128,512]{2,1,0:T(8,128)(2,1)S(1)}, bf16[2,128,128]{2,1,0:T(8,128)(2,1)S(1)}, bf16[2,128,128]{2,1,0:T(8,128)(2,1)S(1)}) custom-call(bf16[2,128,512]{2,1,0:T(8,128)(2,1)} %q_hbm.1, bf16[2,128,128]{2,1,0:T(8,128)(2,1)} %k_hbm.1, bf16[2,128,128]{2,1,0:T(8,128)(2,1)} %v_hbm.1, ...), custom_call_target="tpu_custom_call" | custom-call | tf_op jit(solution)/shard_map/attention_both_ways/pallas_call | solution.py:403
  12.5 0.9 %store_results.1 = (bf16[2,128,512]{2,1,0:T(8,128)(2,1)}, bf16[2,128,512]{2,1,0:T(8,128)(2,1)}, bf16[2,128,128]{2,1,0:T(8,128)(2,1)}, bf16[2,128,128]{2,1,0:T(8,128)(2,1)}) custom-call(bf16[2,128,512]{2,1,0:T(8,128)(2,1)S(1)} %get-tuple-element.8.refs_0_, bf16[2,128,512]{2,1,0:T(8,128)(2,1)S(1)} %get-tuple-element.9.refs_1_, ...), custom_call_target="tpu_custom_call" | custom-call | tf_op jit(solution)/shard_map/store_results/pallas_call | solution.py:447

commit v8 on v6

--- a/solution.py
+++ b/solution.py
@@ -221,18 +221,17 @@
                 p_low[block, :span] = prob_b
                 s_low[block, :span] = slope_b
             if send:
-                part_v = nn(prob_b, stacked(u_all, pack, block))
-                part_k = nn(slope_b, stacked(q_all, pack, block))
                 if block == 0:
-                    carry_k, carry_v = part_k[tok:], part_v[tok:]
-                    done_k, done_v = part_k[:tok], part_v[:tok]
-                else:
-                    done_k, done_v = carry_k + part_k, carry_v + part_v
-                g_back[pack, block, 0] = done_k.astype(jnp.bfloat16)
-                g_back[pack, block, 1] = done_v.astype(jnp.bfloat16)
-                if block == 0:
+                    far_v, far_k = prob_b[tok:], slope_b[tok:]
+                    g_back[pack, 0, 0] = nn(slope_b[:tok], stacked(q_all, pack, 0)).astype(jnp.bfloat16)
+                    g_back[pack, 0, 1] = nn(prob_b[:tok], stacked(u_all, pack, 0)).astype(jnp.bfloat16)
                     pl.when(chip != 1)(back_copy(pack, 0).start)
                 else:
+                    for n, (rows, far, near) in enumerate(((q_all, far_k, slope_b), (u_all, far_v, prob_b))):
+                        g_back[pack, 1, n] = nn(
+                            jnp.concatenate([far, near], axis=1),
+                            jnp.concatenate([stacked(rows, pack, 0), stacked(rows, pack, 1)], axis=0),
+                        ).astype(jnp.bfloat16)
                     back_copy(pack, 1).start()
                     pl.when(chip == 1)(back_copy(pack, 0).start)
 

time: 13.5 us -> 13.5 us (level)
  no operation moved by 1% of the time
where the time goes in v8:
time: 13.5 us; the launch traced here: 13.4 us
  Pallas kernels  12.7 us (94%)
  between operations  0.64 us (5%)
    pallas_call x1, Pallas kernels, per_device(): pl.pallas_call(kernel, out_shape=tuple((pltpu.VMEM(shape, bf16) for shape...  11.9 us
    pallas_call x1, Pallas kernels, per_device(): pl.pallas_call(store, out_shape=tuple((jax.ShapeDtypeStruct(shape, bf16)...  0.86 us

profile of v8, /device:TPU:1, one launch (start us, length us, event | category | flops | bytes accessed | tf_op | source)
XLA Modules:
  0.0 13.4 jit_solution(7148447569737685530)
XLA Ops:
  0.6 11.9 %attention_both_ways.1 = (bf16[2,128,512]{2,1,0:T(8,128)(2,1)S(1)}, bf16[2,128,512]{2,1,0:T(8,128)(2,1)S(1)}, bf16[2,128,128]{2,1,0:T(8,128)(2,1)S(1)}, bf16[2,128,128]{2,1,0:T(8,128)(2,1)S(1)}) custom-call(bf16[2,128,512]{2,1,0:T(8,128)(2,1)} %q_hbm.1, bf16[2,128,128]{2,1,0:T(8,128)(2,1)} %k_hbm.1, bf16[2,128,128]{2,1,0:T(8,128)(2,1)} %v_hbm.1, ...), custom_call_target="tpu_custom_call" | custom-call | tf_op jit(solution)/shard_map/attention_both_ways/pallas_call | solution.py:395
  12.5 0.9 %store_results.1 = (bf16[2,128,512]{2,1,0:T(8,128)(2,1)}, bf16[2,128,512]{2,1,0:T(8,128)(2,1)}, bf16[2,128,128]{2,1,0:T(8,128)(2,1)}, bf16[2,128,128]{2,1,0:T(8,128)(2,1)}) custom-call(bf16[2,128,512]{2,1,0:T(8,128)(2,1)S(1)} %get-tuple-element.8.refs_0_, bf16[2,128,512]{2,1,0:T(8,128)(2,1)S(1)} %get-tuple-element.9.refs_1_, ...), custom_call_target="tpu_custom_call" | custom-call | tf_op jit(solution)/shard_map/store_results/pallas_call | solution.py:439
